TPU v7x, 32 devices: a whole 2x2x4 slice. The times are simulated.
32 devices in a mesh: dp: 4 (over x, core), mp: 8 (over z, y).
Axes of the slice: x: 2, y: 2, z: 4, core: 2. Of those that a mesh axis runs over, the one named last changes fastest.
Arguments:
- prelude_output: bfloat16 [12, 32, 5280], P('dp', None, 'mp'), may hold values from -6 to 6
- init_noise: bfloat16 [16, 32, 5280], P('dp', None, 'mp'), may hold values from -6 to 6
- core_weight: bfloat16 [5280, 5280], P('mp'), may hold values from -0.078125 to 0.078125
- norm_gain: float32 [5280], replicated, may hold values from 0.5 to 1.5
- state_cotangent: bfloat16 [16, 32, 5280], P('dp', None, 'mp'), may hold values from -6 to 6
- step_counts: int32 [12], replicated, may hold values from 1 to 3, as said below
- group_table: int32 [12], replicated, may hold values from 0 to 3, as said below
Outputs:
- weight_grad: float32 [5280, 5280], P('mp', 'dp')
Inputs may be any that keep to these rules, and one draw needn't show every extreme that they name: `step_counts`: sequences in the groups that run fewer sequences all take 3 steps. `group_table`: half of the groups run 4 sequences and the other half run 2 (their other 2 slots stay empty).
All inputs are finite; a program needn't handle non-finite values.
Results may differ from a plain program's by a relative error of at most 0.025.
Values may be sent and summed in bfloat16 or wider, within the bound.
A program may use at most 64 MiB of HBM per device.

v0:
```python
import jax
import jax.numpy as jnp
from jax import lax
from jax.sharding import PartitionSpec as P

MAXR = 3
BP = 2


EPS = 1e-06


def local(
    prelude_output, init_noise, core_weight, norm_gain, state_cotangent, step_counts, group_table
):
    full_width = core_weight.shape[1]
    local_width = core_weight.shape[0]
    slot_total = init_noise.shape[0]
    seq_length = init_noise.shape[1]
    row_count = slot_total * seq_length
    my_group = lax.axis_index("dp")
    column_first = lax.axis_index("mp") * local_width
    seq_total = group_table.shape[0]
    seq_index = jnp.arange(seq_total, dtype=jnp.int32)
    earlier = (group_table[:, None] == group_table[None, :]) & (
        seq_index[None, :] < seq_index[:, None]
    )
    slot_rank = jnp.sum(earlier.astype(jnp.int32), axis=1)
    selected_rows = (group_table[None, :] == my_group) & (
        slot_rank[None, :] == jnp.arange(slot_total, dtype=jnp.int32)[:, None]
    )
    slot_counts = jnp.sum(jnp.where(selected_rows, step_counts[None, :], 0), axis=1)
    chosen_weights = selected_rows.astype(jnp.bfloat16)
    injected_input = jnp.einsum(
        "br,ref->bef",
        chosen_weights,
        lax.all_gather(prelude_output, "dp", axis=0, tiled=True),
        preferred_element_type=jnp.float32,
    ).reshape(row_count, local_width)
    gain_local = lax.dynamic_slice_in_dim(norm_gain, column_first, local_width, 0)

    def feature_sum(values):
        return lax.psum(values, "mp")

    shard_state = init_noise.reshape(row_count, local_width)
    saved = []
    piece_rows = lax.all_gather(shard_state, "mp", axis=1, tiled=True)
    product = lax.dot_general(
        piece_rows, core_weight, (((1,), (1,)), ((), ())), preferred_element_type=jnp.float32
    )
    whole_state = piece_rows
    product, whole_state = (product, whole_state)
    for turn in range(MAXR):
        active = jnp.repeat(turn >= MAXR - slot_counts, seq_length)[:, None]
        if turn > 0:
            product = lax.dot_general(
                whole_state,
                core_weight,
                (((1,), (1,)), ((), ())),
                preferred_element_type=jnp.float32,
            )
        mixed = (product + injected_input).astype(jnp.bfloat16)
        mixed_float = mixed.astype(jnp.float32)
        if turn + 1 < MAXR:
            mixed_whole = lax.all_gather(mixed, "mp", axis=1, tiled=True).astype(jnp.float32)
            inverse_rms = lax.rsqrt(jnp.sum(mixed_whole * mixed_whole, axis=1) / full_width + EPS)
            renewed = (norm_gain * mixed_whole * inverse_rms[:, None]).astype(jnp.bfloat16)
            saved.append((whole_state, mixed_float, inverse_rms, active))
            whole_state = jnp.where(active, renewed, whole_state)
        else:
            inverse_rms = lax.rsqrt(
                feature_sum(jnp.sum(mixed_float * mixed_float, axis=1)) / full_width + EPS
            )
            saved.append((whole_state, mixed_float, inverse_rms, active))
    upstream = state_cotangent.reshape(row_count, local_width).astype(jnp.float32)
    weight_grad = jnp.zeros((local_width, full_width), jnp.float32)
    for back_index in range(BP):
        whole_state, mixed_float, inverse_rms, active = saved[MAXR - 1 - back_index]
        scaled = upstream * gain_local
        inner = feature_sum(jnp.sum(scaled * mixed_float, axis=1))
        delta = (
            inverse_rms[:, None] * scaled
            - mixed_float * (inverse_rms**3 * inner / full_width)[:, None]
        )
        delta_b = jnp.where(active, delta, 0.0).astype(jnp.bfloat16)
        weight_grad = weight_grad + lax.dot_general(
            delta_b, whole_state, (((0,), (0,)), ((), ())), preferred_element_type=jnp.float32
        )
        if back_index + 1 < BP:
            partial_rows = jnp.dot(delta_b, core_weight, preferred_element_type=jnp.float32)
            summed_rows = lax.psum_scatter(
                partial_rows.astype(jnp.bfloat16), "mp", scatter_dimension=1, tiled=True
            ).astype(jnp.float32)
            upstream = jnp.where(active, summed_rows, upstream)
    return lax.psum_scatter(
        weight_grad.astype(jnp.bfloat16), "dp", scatter_dimension=1, tiled=True
    ).astype(jnp.float32)


def solution(mesh):
    return jax.shard_map(
        local,
        mesh=mesh,
        in_specs=(
            P("dp", None, "mp"),
            P("dp", None, "mp"),
            P("mp", None),
            P(),
            P("dp", None, "mp"),
            P(),
            P(),
        ),
        out_specs=P("mp", "dp"),
        check_vma=False,
    )
```

profile of v0, /device:TPU:0, one launch (start us, length us, event | category | flops | bytes accessed | tf_op | source)
XLA Modules:
  0.0 356.4 jit_solution(9886979294357783250)
XLA Ops:
  6.5 1.7 copy.36
  8.3 0.0 all-gather.7.cloned.1.call-update
  8.3 0.0 all-gather.9.cloned.1.call-start
  8.3 0.9 convert_reduce_fusion
  9.3 9.2 %all_gather.13 = bf16[12,32,660]{2,1,0:T(8,128)(2,1)S(1)} all-gather(bf16[3,32,660]{2,1,0:T(8,128)(2,1)} %param.7), channel_id=1, replica_groups=mesh['dp'=4,'mp'=8] {'dp'}, dimensions={0}, use_global_device_ids=true | all-gather | bytes 633600 | tf_op jit(solution)/shard_map/all_gather | solution.py:37
  18.4 0.7 broadcast_compare_fusion.3
  19.1 0.4 fusion.10
  19.5 0.1 copy.38
  19.6 0.2 copy.39
  19.8 34.9 %all-gather.7.cloned.1.call-done = bf16[8,660,128]{2,1,0:T(8,128)(2,1)} async-done(((bf16[1,660,128]{2,1,0:T(8,128)(2,1)}), bf16[8,660,128]{2,1,0:T(8,128)(2,1)}) %all-gather.7.cloned.1.call-update) | async-done | bytes 1351696 | tf_op jit(solution)/shard_map/all_gather | solution.py:47
  54.7 1.4 reshape.37
  56.2 0.0 copy-start.2
  56.2 0.0 copy-start.13
  56.2 6.2 %fusion.9 = bf16[1,660,128]{2,1,0:T(8,128)(2,1)} fusion(f32[128,660]{0,1:T(8,128)S(1)} %copy.39, bf16[5280,128]{1,0:T(8,128)(2,1)S(1)} %reshape.37, bf16[660,5280]{1,0:T(8,128)(2,1)} %param.9), kind=kOutput, calls=%fused_computation.17 | convolution fusion | flops 892277760 | bytes 8828160 | tf_op jit(solution)/shard_map/dot_general | solution.py:48
  62.4 0.0 all-gather.9.cloned.1.call-update
  62.4 0.0 all-gather.11.cloned.1.call-start
  62.5 0.1 select_reduce_fusion
  62.6 0.1 broadcast_in_dim.90
  62.7 0.1 broadcast_in_dim.91
  62.8 40.9 %all-gather.9.cloned.1.call-done = bf16[8,660,128]{2,1,0:T(8,128)(2,1)} async-done(((bf16[1,660,128]{2,1,0:T(8,128)(2,1)}), bf16[8,660,128]{2,1,0:T(8,128)(2,1)}) %all-gather.9.cloned.1.call-update) | async-done | bytes 1351696 | tf_op jit(solution)/shard_map/all_gather | solution.py:65
  103.7 1.4 reshape.42
  105.1 0.0 copy-start.3
  105.1 0.7 multiply_reduce_fusion.1
  105.8 0.0 copy-done.11
  105.9 0.6 copy-done.3
  106.4 2.2 fusion.2
  108.7 0.0 copy-done.6
  108.7 0.0 copy-start.10
  108.7 0.0 copy-start.12
  108.7 6.3 %fusion.6 = bf16[128,660]{0,1:T(8,128)(2,1)} fusion(f32[128,660]{0,1:T(8,128)S(1)} %copy.39, bf16[128,5280]{0,1:T(8,128)(2,1)S(1)} %fusion.2, bf16[660,5280]{1,0:T(8,128)(2,1)} %param.9), kind=kOutput, calls=%fused_computation.14 | convolution fusion | flops 892277760 | bytes 8828160 | tf_op jit(solution)/shard_map/dot_general | solution.py:56
  115.0 0.0 all-gather.11.cloned.1.call-update
  115.0 0.0 reduce-scatter.6.cloned.1.call-start
  115.1 0.1 broadcast_in_dim.84
  115.2 0.1 broadcast_in_dim.85
  115.2 0.1 broadcast_in_dim.87
  115.3 0.1 broadcast_in_dim.88
  115.4 0.1 dynamic_slice.3
  115.5 0.8 bitcast_convert_fusion
  116.3 1.3 copy.42
  117.6 0.6 dynamic-slice.4
  118.8 37.4 %all-gather.11.cloned.1.call-done = bf16[8,660,128]{2,1,0:T(8,128)(2,1)} async-done(((bf16[1,660,128]{2,1,0:T(8,128)(2,1)}), bf16[8,660,128]{2,1,0:T(8,128)(2,1)}) %all-gather.11.cloned.1.call-update) | async-done | bytes 1351696 | tf_op jit(solution)/shard_map/all_gather | solution.py:65
  156.3 2.7 reshape.43
  159.0 2.6 multiply_reduce_fusion
  161.6 3.8 %fusion.4 = bf16[128,5280]{0,1:T(8,128)(2,1)S(1)} fusion(bf16[128,5280]{0,1:T(8,128)(2,1)} %copy-done, f32[5280,128]{1,0:T(8,128)} %reshape.43, f32[128]{0:T(128)S(1)} %add_rsqrt_fusion.1, f32[5280]{0:T(1024)S(1)} %copy-done.11, pred[128]{0:T(512)(128)(4,1)S(1)} %broadcast_in_dim.88), kind=kLoop, calls=%fused_computation.9 | loop fusion | flops 2703360 | bytes 5428480 | tf_op jit(solution)/shard_map/jit(_where)/select_n | solution.py:69
  165.5 0.0 copy-start.4
  165.5 2.8 multiply_reduce_fusion.3
  168.3 19.3 %all-reduce.2 = (f32[128]{0:T(128)S(1)}, f32[128]{0:T(128)S(1)}) all-reduce(f32[128]{0:T(128)S(1)} %get-tuple-element.6, f32[128]{0:T(128)S(1)} %get-tuple-element.5), channel_id=1, replica_groups=mesh['dp'=4,'mp'=8] {'mp'}, use_global_device_ids=true, to_apply=%region_7.8 | all-reduce | flops 256 | bytes 2048 | tf_op jit(solution)/shard_map/psum | solution.py:43
  187.6 1.1 select_convert_fusion
  188.8 0.0 copy-start.5
  188.8 6.4 %convolution_convert_fusion = bf16[128,5280]{0,1:T(8,128)(2,1)S(1)} fusion(bf16[128,660]{0,1:T(8,128)(2,1)S(1)} %select_convert_fusion, bf16[660,5280]{1,0:T(8,128)(2,1)} %param.9), kind=kOutput, calls=%fused_computation.1 | convolution fusion | flops 892784640 | bytes 8490240 | tf_op jit(solution)/shard_map/dot_general | solution.py:90
  195.2 30.9 %fusion = bf16[128,672]{0,1:T(8,128)(2,1)S(1)} fusion(bf16[128,5280]{0,1:T(8,128)(2,1)S(1)} %convolution_convert_fusion), kind=kCustom, calls=%all-reduce-scatter | all-reduce-scatter fusion | flops 688129 | bytes 1524224
  226.1 0.7 copy-done.9
  226.8 1.4 collective-permute-start
  228.2 7.1 %fusion.36 = f32[660,5280]{1,0:T(8,128)} fusion(bf16[128,660]{0,1:T(8,128)(2,1)S(1)} %select_convert_fusion, bf16[128,5280]{0,1:T(8,128)(2,1)S(1)} %copy-done.5), kind=kOutput, calls=%fused_computation.63 | convolution fusion | flops 892108800 | bytes 15459840 | tf_op jit(solution)/shard_map/dot_general | solution.py:86
  235.3 0.0 collective-permute-done
  235.3 1.3 concatenate
  236.6 0.2 fusion.12
  236.8 18.1 %psum.23 = f32[128]{0:T(128)S(1)} all-reduce(f32[128]{0:T(128)S(1)} %fusion.12), channel_id=1, replica_groups=mesh['dp'=4,'mp'=8] {'mp'}, use_global_device_ids=true, to_apply=%region_10.11 | all-reduce | flops 128 | bytes 1024 | tf_op jit(solution)/shard_map/psum | solution.py:43
  254.9 10.0 %add_convert_fusion = bf16[660,5280]{1,0:T(8,128)(2,1)} fusion(f32[660,5280]{1,0:T(8,128)} %fusion.36, bf16[128,5280]{0,1:T(8,128)(2,1)S(1)} %copy-done.1, bf16[128,660]{0,1:T(8,128)(2,1)S(1)} %copy-done.8, f32[128,660]{0,1:T(8,128)S(1)} %copy.42, f32[128]{0:T(128)S(1)} %fusion.33, f32[128]{0:T(128)S(1)} %add_rsqrt_fusion.1, f32[660]{0:T(1024)S(1)} %dynamic_slice.3, ...), kind=kOutput, calls=%fused_computation | convolution fusion | flops 899838720 | bytes 22946564 | tf_op jit(solution)/shard_map/dot_general | solution.py:86
  264.9 11.1 %copy.44 = bf16[660,5280]{0,1:T(8,128)(2,1)} copy(bf16[660,5280]{1,0:T(8,128)(2,1)} %add_convert_fusion) | data formatting | bytes 13939200
  276.0 0.0 reduce-scatter.6.cloned.1.call-update
  276.0 68.7 %reduce-scatter.6.cloned.1.call-done = bf16[1320,660]{1,0:T(8,128)(2,1)} async-done(((bf16[5280,660]{1,0:T(8,128)(2,1)}), bf16[1320,660]{1,0:T(8,128)(2,1)}) %reduce-scatter.6.cloned.1.call-update) | async-done | bytes 1742416
  344.7 3.0 copy.45
  347.8 2.1 convert_element_type.72
  (29 shorter events, 0.1 us)
Async XLA Ops:
  6.5 48.2 %all-gather.7.cloned.1.call-start = ((), (), s32[]{:S(2)}) async-start(), calls=%async_computation.1 | async-start | bytes 1529856 | tf_op jit(solution)/shard_map/all_gather | solution.py:47
  8.3 95.4 %all-gather.9.cloned.1.call-start = ((), (), s32[]{:S(2)}) async-start(), calls=%async_computation.2 | async-start | bytes 1529856 | tf_op jit(solution)/shard_map/all_gather | solution.py:65
  19.8 88.9 %copy-start.6 = (f32[128,660]{0,1:T(8,128)}, f32[128,660]{0,1:T(8,128)S(1)}, u32[]{:S(2)}) copy-start(f32[128,660]{0,1:T(8,128)S(1)} %copy.39) | copy-start | bytes 1013764
  56.2 6.2 %copy-start.2 = (bf16[5280,128]{1,0:T(8,128)(2,1)}, bf16[5280,128]{1,0:T(8,128)(2,1)S(1)}, u32[]{:S(2)}) copy-start(bf16[5280,128]{1,0:T(8,128)(2,1)S(1)} %reshape.37) | copy-start | bytes 4055044
  56.2 6.3 %copy-start.13 = (s32[12]{0:T(128)S(1)}, s32[12]{0:T(128)}, u32[]{:S(2)}) copy-start(s32[12]{0:T(128)} %param.12) | copy-start | bytes 148
  62.4 93.9 %all-gather.11.cloned.1.call-start = ((), (), s32[]{:S(2)}) async-start(), calls=%async_computation.3 | async-start | bytes 1529856 | tf_op jit(solution)/shard_map/all_gather | solution.py:65
  62.8 43.1 %copy-start.11 = (f32[5280]{0:T(1024)S(1)}, f32[5280]{0:T(1024)}, u32[]{:S(2)}) copy-start(f32[5280]{0:T(1024)} %param.10) | copy-start | bytes 63364
  105.1 1.3 copy-start.3
  108.7 6.3 %copy-start = (bf16[128,5280]{0,1:T(8,128)(2,1)}, bf16[128,5280]{0,1:T(8,128)(2,1)S(1)}, u32[]{:S(2)}) copy-start(bf16[128,5280]{0,1:T(8,128)(2,1)S(1)} %fusion.2) | copy-start | bytes 4055044
  108.7 6.8 %copy-start.10 = (bf16[4,32,660]{2,1,0:T(8,128)(2,1)S(1)}, bf16[4,32,660]{2,1,0:T(8,128)(2,1)}, u32[]{:S(2)}) copy-start(bf16[4,32,660]{2,1,0:T(8,128)(2,1)} %param.11) | copy-start | bytes 506884
  108.7 8.9 %copy-start.12 = (u32[32]{0:T(128)S(1)}, u32[32]{0:T(128)}, u32[]{:S(2)}) copy-start(u32[32]{0:T(128)} %constant.38) | copy-start | bytes 388
  115.0 229.7 %reduce-scatter.6.cloned.1.call-start = ((), (), s32[]{:S(2)}) async-start(), calls=%async_computation.4 | async-start | bytes 10137600
  116.3 49.2 %slice-start = ((s8[7139328]{0:T(1024)(128)(4,1)}), s8[2945024]{0:T(1024)(128)(4,1)S(1)}, s32[]{:S(2)}) async-start(s8[7139328]{0:T(1024)(128)(4,1)} %bitcast.45), calls=%async_computation.5 | async-start | bytes 5890048
  159.0 6.5 %slice-start.1 = ((s8[7139328]{0:T(1024)(128)(4,1)}), s8[4194304]{0:T(1024)(128)(4,1)S(1)}, s32[]{:S(2)}) async-start(s8[7139328]{0:T(1024)(128)(4,1)} %bitcast.45), calls=%async_computation.6 | async-start | bytes 8388608
  161.6 3.9 %copy-start.7 = (f32[128,660]{0,1:T(8,128)S(1)}, f32[128,660]{0,1:T(8,128)}, u32[]{:S(2)}) copy-start(f32[128,660]{0,1:T(8,128)} %copy-done.6) | copy-start | bytes 1013764
  165.5 2.8 copy-start.4
  188.8 39.4 %copy-start.5 = (bf16[128,5280]{0,1:T(8,128)(2,1)S(1)}, bf16[128,5280]{0,1:T(8,128)(2,1)}, u32[]{:S(2)}) copy-start(bf16[128,5280]{0,1:T(8,128)(2,1)} %copy-done.4) | copy-start | bytes 4055044
  226.1 0.7 copy-start.9
  226.7 9.9 %copy-start.8 = (bf16[128,660]{0,1:T(8,128)(2,1)S(1)}, bf16[128,660]{0,1:T(8,128)(2,1)}, u32[]{:S(2)}) copy-start(bf16[128,660]{0,1:T(8,128)(2,1)} %fusion.6) | copy-start | bytes 506884
  226.7 28.2 %copy-start.1 = (bf16[128,5280]{0,1:T(8,128)(2,1)S(1)}, bf16[128,5280]{0,1:T(8,128)(2,1)}, u32[]{:S(2)}) copy-start(bf16[128,5280]{0,1:T(8,128)(2,1)} %copy-done) | copy-start | bytes 4055044
  226.8 8.6 %collective-permute-start = (bf16[128,84]{0,1:T(8,128)(2,1)S(1)}, bf16[128,84]{0,1:T(8,128)(2,1)S(1)}, u32[]{:S(2)}, u32[]{:S(2)}) collective-permute-start(bf16[128,84]{0,1:T(8,128)(2,1)S(1)} %slice), channel_id=1, source_target_pairs={{0,1},{1,2},{2,3},{3,4},{4,5},{5,6},{6,7},{8,9},{9,10},{10,11},{11... | collective-permute-start | bytes 64520
Sparse Core Ops, SparseCore 0:
  9.5 45.1 all-gather.6
  62.5 41.0 all-gather.8
  115.1 41.0 all-gather.10
  276.1 68.5 reduce-scatter.5
where the time goes:
time: 357 us; the launch traced here: 356 us
  waiting for transfers between devices  182 us (51%)
  blocking collectives  77.4 us (22%)
  matrix products  39.2 us (11%)
  local copies, waits for them, and re-layouts  26.7 us (7%)
  other arithmetic  15.4 us (4%)
  between operations  14.1 us (4%)
    all_gather x2, waiting for transfers between devices, local(): lax.all_gather(mixed, 'mp', axis=1, tiled=True).astype(jnp.float32)  78.3 us
    unnamed x6, waiting for transfers between devices  68.8 us
    psum x2, blocking collectives, feature_sum(): return lax.psum(values, 'mp')  37.4 us
    all_gather x1, waiting for transfers between devices, local(): piece_rows = lax.all_gather(shard_state, 'mp', axis=1, tiled=True)  34.9 us
    unnamed x1, blocking collectives  30.9 us
    unnamed x39, local copies, waits for them, and re-layouts  20.5 us
    dot_general x2, matrix products, local(): lax.dot_general(delta_b, whole_state, (((0,), (0,)), ((), ())), preferred...  17.1 us
    all_gather x1, blocking collectives, local(): lax.all_gather(prelude_output, 'dp', axis=0, tiled=True)  9.18 us
  transfers between devices with their start and end apart: 5, of which 4 were waited for; matrix products, arithmetic and copies ran while one was open for 4% of the time, Pallas kernels for 0%

commit v1 on v0

--- a/solution.py
+++ b/solution.py
@@ -1,8 +1,17 @@
+import functools
+
 import jax
 import jax.numpy as jnp
 from jax import lax
+from jax.experimental import pallas as pl
+from jax.experimental.pallas import tpu as pltpu
 from jax.sharding import PartitionSpec as P
 
+MESH = pl.DeviceIdType.MESH
+NT = (((1,), (1,)), ((), ()))
+TN = (((0,), (0,)), ((), ()))
+F32 = jnp.float32
+BF16 = jnp.bfloat16
 MAXR = 3
 BP = 2
 
@@ -97,9 +106,443 @@
     ).astype(jnp.float32)
 
 
+def core_kernel(
+    n_dp, n_mp, full_width,
+    pick_ref, own_ref, part_ref, prelude_ref, noise_ref, cot_ref, counts_ref, gain_ref, w_hbm,
+    out_ref,
+    w_ref, w8, u0, u1, u2, y0, y1, xs, ds, inject, acc, square, cot_rows, scaled, delta_b,
+    pre_all, noise_all, cot_all, red, pair_send, pair_recv, line_send, line_recv,
+    w_sem, in_send, in_recv, g_send, g_recv, x_send, x_recv, d_send, d_recv,
+    red_send, red_recv, p_send, p_recv, l_send, l_recv,
+):
+    dp = lax.axis_index("dp")
+    mp = lax.axis_index("mp")
+    n_line = n_mp // 2
+    line, side = mp // 2, lax.rem(mp, 2)
+    blocks = n_mp // n_dp
+    seq_dev, tokens, width = prelude_ref.shape
+    rows = seq_dev * tokens
+
+    w_copy = pltpu.make_async_copy(w_hbm, w_ref, w_sem)
+    w_copy.start()
+
+    barrier = pltpu.get_barrier_semaphore()
+    for o in range(1, n_mp):
+        pl.semaphore_signal(
+            barrier, inc=1, device_id=(dp, lax.rem(mp + o, n_mp)), device_id_type=MESH
+        )
+    for o in range(1, n_dp):
+        pl.semaphore_signal(
+            barrier, inc=1, device_id=(lax.rem(dp + o, n_dp), mp), device_id_type=MESH
+        )
+    pl.semaphore_wait(barrier, n_mp + n_dp - 2)
+
+    def remote(src, dst, send, recv, device):
+        return pltpu.make_async_remote_copy(
+            src_ref=src, dst_ref=dst, send_sem=send, recv_sem=recv,
+            device_id=device, device_id_type=MESH,
+        )
+
+    in_copies = []
+    for which, (src, dst) in enumerate(
+        ((noise_ref.at[seq_dev], noise_all), (prelude_ref, pre_all), (cot_ref.at[seq_dev], cot_all))
+    ):
+        copies = []
+        for o in range(1, n_dp):
+            copy = remote(
+                src, dst.at[dp], in_send.at[which, o], in_recv.at[which, o],
+                (lax.rem(dp + o, n_dp), mp),
+            )
+            copy.start()
+            copies.append(copy)
+        in_copies.append(copies)
+    noise_all[dp] = noise_ref[seq_dev]
+    cot_all[dp] = cot_ref[seq_dev]
+    pre_all[dp] = prelude_ref[...]
+
+    def third_rows(own, gathered):
+        total = own_ref[0] * own[seq_dev - 1].astype(F32)
+        return lax.fori_loop(
+            0, n_dp, lambda q, t: t + part_ref[q] * gathered[q].astype(F32), total
+        )
+
+    kept = (seq_dev - 1) * tokens
+    for b in range(seq_dev - 1):
+        u0[mp, pl.ds(b * tokens, tokens)] = noise_ref[b]
+    for copy in in_copies[0]:
+        copy.wait_recv()
+    u0[mp, pl.ds(kept, tokens)] = third_rows(noise_ref, noise_all).astype(BF16)
+
+    peer = (dp, line * 2 + 1 - side)
+
+    def gather_start(turn, buf):
+        own = buf.at[mp]
+        remote(own, own, g_send.at[turn, 1], g_recv.at[turn, 1], peer).start()
+        for h in range(1, n_line):
+            to = (dp, lax.rem(line + h, n_line) * 2 + side)
+            remote(own, own, g_send.at[turn, 1 + h], g_recv.at[turn, 1 + h], to).start()
+
+    def gather_steps(turn, buf, use):
+        def step(s, carry):
+            h = jnp.where(s < 2, 0, jnp.where(s <= n_line, s - 1, s - n_line))
+            other = jnp.where(s < 2, s, jnp.where(s <= n_line, 0, 1))
+            from_line = lax.rem(line + n_line - h, n_line)
+            owner = from_line * 2 + lax.rem(side + other, 2)
+
+            @pl.when(s > 0)
+            def _():
+                remote(
+                    buf.at[owner], buf.at[owner], g_send.at[turn, s], g_recv.at[turn, s], peer
+                ).wait_recv()
+
+            @pl.when((s >= 2) & (s <= n_line))
+            def _():
+                f = n_line + s - 1
+                remote(
+                    buf.at[owner], buf.at[owner], g_send.at[turn, f], g_recv.at[turn, f], peer
+                ).start()
+
+            use(owner)
+            return carry
+
+        lax.fori_loop(0, n_mp, step, 0)
+
+    def gather_end(turn, buf):
+        def step(s, carry):
+            remote(
+                buf.at[mp], buf.at[mp], g_send.at[turn, s], g_recv.at[turn, s], peer
+            ).wait_send()
+            return carry
+
+        lax.fori_loop(1, n_mp, step, 0)
+
+    gather_start(0, u0)
+    w_copy.wait()
+    for k in range(n_mp):
+        w8[k] = w_ref[:, k * width : (k + 1) * width]
+
+    counts = counts_ref[...]
+
+    def active(turn):
+        return counts >= float(MAXR - turn)
+
+    acc[...] = jnp.zeros_like(acc)
+
+    def use_first(k):
+        acc[...] += lax.dot_general(u0[k], w8[k], NT, preferred_element_type=F32)
+
+    gather_steps(0, u0, use_first)
+
+    for copy in in_copies[1]:
+        copy.wait_recv()
+    for b in range(seq_dev):
+
+        def add(q, t):
+            for i in range(seq_dev):
+                t = t + pick_ref[b * n_dp * seq_dev + q * seq_dev + i] * pre_all[q, i].astype(F32)
+            return t
+
+        inject[pl.ds(b * tokens, tokens)] = lax.fori_loop(
+            0, n_dp, add, jnp.zeros((tokens, width), F32)
+        )
+
+    def renew(turn, y_all, before, after):
+        live = active(turn)
+        acc[...] = jnp.zeros_like(acc)
+        square[...] = jnp.zeros_like(square)
+
+        def use(k):
+            y = y_all[k].astype(F32)
+            square[...] += jnp.sum(y * y, axis=1, keepdims=True)
+            new = jnp.where(live, gain_ref[k] * y, before[k].astype(F32)).astype(BF16)
+            after[k] = new
+            acc[...] += lax.dot_general(new, w8[k], NT, preferred_element_type=F32)
+            to = k // blocks
+            part = lax.rem(k, blocks)
+
+            @pl.when(to == dp)
+            def _():
+                xs[turn, dp, part] = after[k]
+
+            @pl.when(to != dp)
+            def _():
+                remote(
+                    after.at[k], xs.at[turn, dp, part], x_send.at[turn, k],
+                    x_recv.at[turn, dp, part], (to, mp),
+                ).start()
+
+        gather_steps(1 + turn, y_all, use)
+        return lax.rsqrt(square[...] / full_width + EPS)
+
+    y0[mp] = (acc[...] + inject[...]).astype(BF16)
+    gather_start(1, y0)
+    for copy in in_copies[2]:
+        copy.wait_recv()
+    cot_rows[pl.ds(kept, tokens)] = third_rows(cot_ref, cot_all)
+    for b in range(seq_dev - 1):
+        cot_rows[pl.ds(b * tokens, tokens)] = cot_ref[b].astype(F32)
+    rms0 = renew(0, y0, u0, u1)
+    scale1 = jnp.where(active(0), rms0, 1.0)
+
+    y1[mp] = (scale1 * acc[...] + inject[...]).astype(BF16)
+    gather_start(2, y1)
+    rms1 = renew(1, y1, u1, u2)
+    scale2 = jnp.where(active(1), rms1, scale1)
+    y2 = (scale2 * acc[...] + inject[...]).astype(BF16).astype(F32)
+
+    def all_sums(which, first, second):
+        ones = jnp.ones((4, width), F32)
+
+        def row_sum(values):
+            return lax.dot_general(
+                ones, values, NT, preferred_element_type=F32, precision=lax.Precision.HIGHEST
+            )
+
+        red[which, mp] = jnp.concatenate([row_sum(first), row_sum(second)], axis=0)
+        copies = []
+        for o in range(1, n_mp):
+            copy = remote(
+                red.at[which, mp], red.at[which, mp], red_send.at[which, o],
+                red_recv.at[which, o], (dp, lax.rem(mp + o, n_mp)),
+            )
+            copy.start()
+            copies.append(copy)
+        for copy in copies:
+            copy.wait_recv()
+        total = red[which, 0]
+        for k in range(1, n_mp):
+            total = total + red[which, k]
+        columns = jnp.transpose(total)
+        return columns[:, 0:1], columns[:, 4:5], copies
+
+    gain = gain_ref[mp]
+    scaled[...] = cot_rows[...] * gain
+    square2, inner2, copies_a = all_sums(0, y2 * y2, scaled[...] * y2)
+    rms2 = lax.rsqrt(square2 / full_width + EPS)
+    delta = jnp.where(
+        active(2), rms2 * scaled[...] - y2 * (rms2 * rms2 * rms2 * inner2 / full_width), 0.0
+    )
+    delta_b[...] = delta.astype(BF16)
+
+    def pair_step(s, carry):
+        to_line = lax.rem(line + s + 1, n_line)
+        product = jnp.dot(
+            delta_b[...], w8[to_line * 2 + 1 - side], preferred_element_type=F32
+        )
+        pair_send[s] = product.astype(BF16)
+        remote(pair_send.at[s], pair_recv.at[s], p_send.at[s], p_recv.at[s], peer).start()
+        return carry
+
+    lax.fori_loop(0, n_line, pair_step, 0)
+
+    dp_pair, dp_side = dp // 2, lax.rem(dp, 2)
+    n_pair = n_dp // 2
+    dp_peer = (dp_pair * 2 + 1 - dp_side, mp)
+
+    def spread_start(which, values):
+        ds[which, dp] = values
+        own = ds.at[which, dp]
+        copies = []
+        for h in range(1, n_pair):
+            to = (lax.rem(dp_pair + h, n_pair) * 2 + dp_side, mp)
+            copies.append(remote(own, own, d_send.at[which, h], d_recv.at[which, h], to))
+        copies.append(remote(own, own, d_send.at[which, 0], d_recv.at[which, 0], dp_peer))
+        for copy in copies:
+            copy.start()
+        return copies
+
+    def spread_forward(which, copies):
+        forwards = []
+        for h in range(1, n_pair):
+            copies[h - 1].wait_recv()
+            held = ds.at[which, lax.rem(dp_pair + n_pair - h, n_pair) * 2 + dp_side]
+            f = n_pair + h
+            copy = remote(held, held, d_send.at[which, f], d_recv.at[which, f], dp_peer)
+            copy.start()
+            forwards.append(copy)
+        return forwards
+
+    def spread_wait(copies, forwards):
+        copies[-1].wait_recv()
+        for copy in forwards:
+            copy.wait_recv()
+
+    spread_a = spread_start(1, (delta * scale2).astype(BF16))
+
+    def line_step(s, carry):
+        to_line = lax.rem(line + s + 1, n_line)
+        product = jnp.dot(delta_b[...], w8[to_line * 2 + side], preferred_element_type=F32)
+        remote(
+            pair_send.at[s], pair_recv.at[s], p_send.at[s], p_recv.at[s], peer
+        ).wait_recv()
+        total = product.astype(BF16).astype(F32) + pair_recv[s].astype(F32)
+        acc[...] = total
+
+        @pl.when(s < n_line - 1)
+        def _():
+            line_send[s] = total.astype(BF16)
+            remote(
+                line_send.at[s], line_recv.at[s], l_send.at[s], l_recv.at[s],
+                (dp, to_line * 2 + side),
+            ).start()
+
+        return carry
+
+    lax.fori_loop(0, n_line, line_step, 0)
+    forwards_a = spread_forward(1, spread_a)
+
+    def x_wait(which):
+        for h in range(1, n_dp):
+            q = lax.rem(dp + h, n_dp)
+            for part in range(blocks):
+                remote(
+                    u1.at[0], xs.at[which, q, part], x_send.at[which, 0],
+                    x_recv.at[which, q, part], (q, mp),
+                ).wait_recv()
+
+    def grad(which, part):
+        left = ds[which].reshape(n_dp * rows, width)
+        right = jnp.concatenate([xs[which, q, part] for q in range(n_dp)], axis=0)
+        return lax.dot_general(left, right, TN, preferred_element_type=F32)
+
+    spread_wait(spread_a, forwards_a)
+    x_wait(1)
+    for part in range(blocks):
+        out_ref[:, part * width : (part + 1) * width] = grad(1, part)
+
+    for s in range(n_line - 1):
+        remote(
+            line_send.at[s], line_recv.at[s], l_send.at[s], l_recv.at[s], peer
+        ).wait_recv()
+        acc[...] += line_recv[s].astype(F32)
+    scaled[...] = jnp.where(active(2), acc[...], cot_rows[...]) * gain
+    y_own = y1[mp].astype(F32)
+    unused, inner1, copies_b = all_sums(1, y_own, scaled[...] * y_own)
+    delta = jnp.where(
+        active(1), rms1 * scaled[...] - y_own * (rms1 * rms1 * rms1 * inner1 / full_width), 0.0
+    )
+    spread_b = spread_start(0, (delta * scale1).astype(BF16))
+    forwards_b = spread_forward(0, spread_b)
+    x_wait(0)
+    spread_wait(spread_b, forwards_b)
+    for part in range(blocks):
+        out_ref[:, part * width : (part + 1) * width] += grad(0, part)
+
+    for copies in in_copies + [copies_a, copies_b, spread_a, forwards_a, spread_b, forwards_b]:
+        for copy in copies:
+            copy.wait_send()
+    for turn, buf in enumerate((u0, y0, y1)):
+        gather_end(turn, buf)
+    for s in range(n_line):
+        remote(
+            pair_send.at[s], pair_recv.at[s], p_send.at[s], p_recv.at[s], peer
+        ).wait_send()
+    for s in range(n_line - 1):
+        remote(
+            line_send.at[s], line_recv.at[s], l_send.at[s], l_recv.at[s], peer
+        ).wait_send()
+    for turn, buf in enumerate((u1, u2)):
+        for h in range(1, n_dp):
+            q = lax.rem(dp + h, n_dp)
+            for part in range(blocks):
+                k = q * blocks + part
+                remote(
+                    buf.at[k], xs.at[turn, dp, part], x_send.at[turn, k],
+                    x_recv.at[turn, dp, part], (q, mp),
+                ).wait_send()
+
+
+def fused(
+    n_dp, n_mp,
+    prelude_output, init_noise, core_weight, norm_gain, state_cotangent, step_counts, group_table,
+):
+    width, full_width = core_weight.shape
+    seq_dev, tokens = prelude_output.shape[:2]
+    cap = init_noise.shape[0]
+    rows = seq_dev * tokens
+    blocks = n_mp // n_dp
+    dp = lax.axis_index("dp")
+    seqs = group_table.shape[0]
+    index = jnp.arange(seqs, dtype=jnp.int32)
+    groups = jnp.arange(n_dp, dtype=jnp.int32)
+    same = group_table[:, None] == group_table[None, :]
+    rank = jnp.sum((same & (index[None, :] < index[:, None])).astype(jnp.int32), axis=1)
+    sizes = jnp.sum((group_table[None, :] == groups[:, None]).astype(jnp.int32), axis=1)
+    full = sizes == cap
+    mine_full = jnp.sum(jnp.where(groups == dp, full, False).astype(jnp.int32)) > 0
+    earlier = groups[None, :] < groups[:, None]
+    order = jnp.sum((earlier & (full[None, :] == full[:, None])).astype(jnp.int32), axis=1)
+    mine_order = jnp.sum(jnp.where(groups == dp, order, 0))
+    part = full & (order == mine_order) & ~mine_full
+    partner = jnp.sum(jnp.where(part, groups, 0))
+    place = jnp.arange(seq_dev, dtype=jnp.int32)
+    moved = (place == seq_dev - 1) & ~mine_full
+    want_group = jnp.where(moved, partner, dp)
+    want_rank = jnp.where(moved, cap - 1, place)
+    pick = (group_table[None, :] == want_group[:, None]) & (rank[None, :] == want_rank[:, None])
+    counts = jnp.sum(jnp.where(pick, step_counts[None, :], 0), axis=1)
+    row_counts = jnp.repeat(counts.astype(F32), tokens)[:, None]
+    vmem = pl.BlockSpec(memory_space=pltpu.VMEM)
+    smem = pl.BlockSpec(memory_space=pltpu.SMEM)
+    state = pltpu.VMEM((n_mp, rows, width), BF16)
+    row_f32 = pltpu.VMEM((rows, width), F32)
+    n_line, n_pair = n_mp // 2, n_dp // 2
+    dma = pltpu.SemaphoreType.DMA
+    scratch = [
+        pltpu.VMEM((width, full_width), BF16),
+        pltpu.VMEM((n_mp, width, width), BF16),
+        state, state, state, state, state,
+        pltpu.VMEM((BP, n_dp, blocks, rows, width), BF16),
+        pltpu.VMEM((BP, n_dp, rows, width), BF16),
+        row_f32, row_f32, pltpu.VMEM((rows, 1), F32), row_f32, row_f32,
+        pltpu.VMEM((rows, width), BF16),
+        pltpu.VMEM((n_dp, seq_dev, tokens, width), BF16),
+        pltpu.VMEM((n_dp, tokens, width), BF16),
+        pltpu.VMEM((n_dp, tokens, width), BF16),
+        pltpu.VMEM((BP, n_mp, 8, rows), F32),
+        pltpu.VMEM((n_line, rows, width), BF16),
+        pltpu.VMEM((n_line, rows, width), BF16),
+        pltpu.VMEM((n_line, rows, width), BF16),
+        pltpu.VMEM((n_line, rows, width), BF16),
+        dma,
+        dma((3, n_dp)), dma((3, n_dp)),
+        dma((MAXR, n_mp)), dma((MAXR, n_mp)),
+        dma((BP, n_mp)), dma((BP, n_dp, blocks)),
+        dma((BP, 2 * n_pair)), dma((BP, 2 * n_pair)),
+        dma((BP, n_mp)), dma((BP, n_mp)),
+        dma((n_line,)), dma((n_line,)),
+        dma((n_line,)), dma((n_line,)),
+    ]
+    return pl.pallas_call(
+        functools.partial(core_kernel, n_dp, n_mp, full_width),
+        out_shape=jax.ShapeDtypeStruct((width, blocks * width), F32),
+        in_specs=[smem] * 3 + [vmem] * 5 + [pl.BlockSpec(memory_space=pl.ANY)],
+        out_specs=vmem,
+        scratch_shapes=scratch,
+        compiler_params=pltpu.CompilerParams(
+            collective_id=0, has_side_effects=True, vmem_limit_bytes=56 * 1024 * 1024
+        ),
+        cost_estimate=pl.CostEstimate(
+            flops=2 * rows * full_width * width * 8, bytes_accessed=20_000_000, transcendentals=0
+        ),
+    )(
+        pick.astype(F32).reshape(-1),
+        mine_full.astype(F32).reshape(1),
+        part.astype(F32),
+        prelude_output,
+        init_noise,
+        state_cotangent,
+        row_counts,
+        norm_gain.reshape(n_mp, 1, width),
+        core_weight,
+    )
+
+
 def solution(mesh):
+    n_dp, n_mp = mesh.shape["dp"], mesh.shape["mp"]
+    paired = n_mp % n_dp == 0 and n_mp % 2 == 0 and n_dp % 2 == 0
     return jax.shard_map(
-        local,
+        functools.partial(fused, n_dp, n_mp) if paired else local,
         mesh=mesh,
         in_specs=(
             P("dp", None, "mp"),

time: 357 us -> 120 us (0.34)
  waiting for transfers between devices: 182 us -> 0 us
  Pallas kernels: 0 us -> 105 us
  blocking collectives: 77.4 us -> 0 us
  matrix products: 39.2 us -> 0 us
  local copies, waits for them, and re-layouts: 26.7 us -> 7.05 us
  between operations: 14.1 us -> 0.73 us
  other arithmetic: 15.4 us -> 5.92 us
    all_gather x3 -> x0, waiting for transfers between devices: 113 us -> none  [the longest x2 78.3 us: local(): lax.all_gather(mixed, 'mp', axis=1, tiled=True).astype(jnp.float32)]
    pallas_call x0 -> x1, Pallas kernels: none -> 105 us  [fused(): pl.pallas_call(functools.partial(core_kernel, n_dp, n_mp, full_width), ou...]
    unnamed x6 -> x0, waiting for transfers between devices: 68.8 us -> none
    dot_general x7 -> x0, matrix products: 39.2 us -> none  [the longest x2 17.1 us: local(): lax.dot_general(delta_b, whole_state, (((0,), (0,)), ((), ())), preferred...]
    psum x2 -> x0, blocking collectives: 37.4 us -> none  [feature_sum(): return lax.psum(values, 'mp')]
    unnamed x1 -> x0, blocking collectives: 30.9 us -> none
    unnamed x39 -> x1, local copies, waits for them, and re-layouts: 20.5 us -> 4.16 us
    all_gather x1 -> x0, blocking collectives: 9.18 us -> none  [local(): lax.all_gather(prelude_output, 'dp', axis=0, tiled=True)]
  transfers between devices with their start and end apart: 5 -> 0, of which waited for: 4 -> 0; matrix products, arithmetic and copies ran while one was open for 4% -> 0% of each run, Pallas kernels for 0% -> 0%
where the time goes in v1:
time: 120 us; the launch traced here: 119 us
  Pallas kernels  105 us (88%)
  local copies, waits for them, and re-layouts  7.05 us (6%)
  other arithmetic  5.92 us (5%)
    pallas_call x1, Pallas kernels, fused(): pl.pallas_call(functools.partial(core_kernel, n_dp, n_mp, full_width), ou...  105 us
    unnamed x1, local copies, waits for them, and re-layouts  4.16 us

profile of v1, /device:TPU:0, one launch (start us, length us, event | category | flops | bytes accessed | tf_op | source)
XLA Modules:
  0.0 118.8 jit_solution(1938155501428930913)
XLA Ops:
  0.0 0.8 convert_reduce_fusion.2
  0.8 0.2 convert_reduce_fusion.1
  1.0 0.9 convert_reduce_fusion
  1.9 0.7 fusion.2
  3.3 1.2 fusion.4
  4.5 0.6 select_reduce_fusion.1
  5.1 0.6 broadcast_select_fusion
  5.8 0.9 select_reduce_fusion
  6.6 0.1 broadcast_in_dim.58
  6.7 0.7 reshape.42.pick_ref
  7.4 1.4 %reshape.41.gain_ref = f32[8,1,660]{2,1,0:T(1,128)} reshape(f32[5280]{0:T(1024)} %param.10) | data formatting | bytes 42240 | tf_op jit(solution)/shard_map/reshape | solution.py:536
  8.8 0.7 broadcast_in_dim_reshape.4.counts_ref
  9.5 105.1 %shard_map.73 = f32[660,1320]{1,0:T(8,128)} custom-call(f32[36]{0:T(128)} %reshape.42.pick_ref, f32[1]{0:T(128)} %bitcast.own_ref, f32[4]{0:T(128)} %get-tuple-element.7.part_ref, bf16[3,32,660]{2,1,0:T(8,128)(2,1)} %prelude_ref.1, bf16[4,32,660]{2,1,0:T(8,128)(2,1)} %noise_ref.1, bf16[4,32,660]{2,1,0:T(8,128)(2,1)} %cot_ref.1, ...), custom_call_target="tpu_custom_call" | custom-call | flops 5352652800 | bytes 20000000 | tf_op jit(solution)/shard_map/pallas_call | solution.py:516
  114.6 4.2 %copy.11 = f32[660,1320]{1,0:T(8,128)} copy(f32[660,1320]{1,0:T(8,128)} %shard_map.73) | data formatting | bytes 6969600
  (4 shorter events, 0.0 us)

commit v2 on v0

--- a/solution.py
+++ b/solution.py
@@ -1,8 +1,18 @@
+import functools
+
 import jax
 import jax.numpy as jnp
 from jax import lax
+from jax.experimental import pallas as pl
+from jax.experimental.pallas import tpu as pltpu
 from jax.sharding import PartitionSpec as P
 
+MESH = pl.DeviceIdType.MESH
+NT = (((1,), (1,)), ((), ()))
+TN = (((0,), (0,)), ((), ()))
+STREAMS = 2
+F32 = jnp.float32
+BF16 = jnp.bfloat16
 MAXR = 3
 BP = 2
 
@@ -97,9 +107,567 @@
     ).astype(jnp.float32)
 
 
+def core_kernel(
+    n_dp, n_mp, streams, full_width, cap,
+    counts_in, groups_in, prelude_ref, noise_ref, cot_ref, gain_in, w_hbm,
+    ds, xs,
+    w_ref, w8, u0, u1, u2, y0, y1, gain_ref, counts_ref, pick_ref, inject, acc, square, scale, rms,
+    cot_rows, scaled, y_last, delta_b, spread_own, total_ref, noise_rows,
+    pre_all, noise_all, cot_all, red, pair_send, pair_recv, line_send, line_recv,
+    w_sem, in_send, in_recv, g_send, g_recv, x_send, x_recv, own_sem, d_send, d_recv,
+    red_send, red_recv, p_send, p_recv, l_send, l_recv,
+):
+    dp = lax.axis_index("dp")
+    mp = lax.axis_index("mp")
+    n_line = n_mp // 2
+    line, side = mp // 2, lax.rem(mp, 2)
+    blocks = n_mp // n_dp
+    seq_dev, tokens, width = prelude_ref.shape
+    rows = seq_dev * tokens
+    part_rows = rows // streams
+
+    w_copy = pltpu.make_async_copy(w_hbm, w_ref, w_sem)
+    w_copy.start()
+
+    barrier = pltpu.get_barrier_semaphore()
+    for o in range(1, n_mp):
+        pl.semaphore_signal(
+            barrier, inc=1, device_id=(dp, lax.rem(mp + o, n_mp)), device_id_type=MESH
+        )
+    for o in range(1, n_dp):
+        pl.semaphore_signal(
+            barrier, inc=1, device_id=(lax.rem(dp + o, n_dp), mp), device_id_type=MESH
+        )
+
+    seqs = groups_in.shape[0]
+    one, zero = jnp.int32(1), jnp.int32(0)
+    group = [groups_in[i] for i in range(seqs)]
+    rank = []
+    for i in range(seqs):
+        r = zero
+        for j in range(i):
+            r = r + jnp.where(group[j] == group[i], one, zero)
+        rank.append(r)
+    full = []
+    for g in range(n_dp):
+        size = zero
+        for i in range(seqs):
+            size = size + jnp.where(group[i] == g, one, zero)
+        full.append(jnp.where(size == cap, one, zero))
+    order = []
+    for g in range(n_dp):
+        r = zero
+        for e in range(g):
+            r = r + jnp.where(full[e] == full[g], one, zero)
+        order.append(r)
+    mine_full, mine_order = zero, zero
+    for g in range(n_dp):
+        mine_full = jnp.where(dp == g, full[g], mine_full)
+        mine_order = jnp.where(dp == g, order[g], mine_order)
+    partner = zero
+    part_weight = []
+    for g in range(n_dp):
+        hit = full[g] * (one - mine_full) * jnp.where(order[g] == mine_order, one, zero)
+        partner = partner + hit * g
+        part_weight.append(hit.astype(F32))
+    own_weight = mine_full.astype(F32)
+    for b in range(seq_dev):
+        want_group, want_rank = dp, jnp.int32(b)
+        if b == seq_dev - 1:
+            want_group = jnp.where(mine_full == one, dp, partner)
+            want_rank = jnp.where(mine_full == one, want_rank, cap - 1)
+        count = zero
+        for i in range(seqs):
+            hit = jnp.where(group[i] == want_group, one, zero) * jnp.where(
+                rank[i] == want_rank, one, zero
+            )
+            count = count + hit * counts_in[i]
+            pick_ref[b * seqs + i] = hit.astype(F32)
+        counts_ref[pl.ds(b * tokens, tokens)] = jnp.zeros((tokens, 1), F32) + count.astype(F32)
+
+    pl.semaphore_wait(barrier, n_mp + n_dp - 2)
+
+    def remote(src, dst, send, recv, device):
+        return pltpu.make_async_remote_copy(
+            src_ref=src, dst_ref=dst, send_sem=send, recv_sem=recv,
+            device_id=device, device_id_type=MESH,
+        )
+
+    in_copies = []
+
+    def cross(which, src, dst):
+        copies = []
+        for o in range(1, n_dp):
+            copy = remote(
+                src, dst.at[dp], in_send.at[which, o], in_recv.at[which, o],
+                (lax.rem(dp + o, n_dp), mp),
+            )
+            copy.start()
+            copies.append(copy)
+        in_copies.append(copies)
+
+    cross(0, noise_ref.at[seq_dev], noise_all)
+    peer = (dp, line * 2 + 1 - side)
+
+    def gather_start(turn, s, buf):
+        own = buf.at[s, mp]
+        remote(own, own, g_send.at[turn, s, 1], g_recv.at[turn, s, 1], peer).start()
+        for h in range(1, n_line):
+            to = (dp, lax.rem(line + h, n_line) * 2 + side)
+            remote(own, own, g_send.at[turn, s, 1 + h], g_recv.at[turn, s, 1 + h], to).start()
+
+    def gather_wait(turn, s, buf, at, owner):
+        remote(
+            buf.at[s, owner], buf.at[s, owner], g_send.at[turn, s, at], g_recv.at[turn, s, at], peer
+        ).wait_recv()
+
+    def gather_forward(turn, s, buf, h):
+        owner = lax.rem(line + n_line - h, n_line) * 2 + side
+        gather_wait(turn, s, buf, 1 + h, owner)
+        at = n_line + h
+        remote(
+            buf.at[s, owner], buf.at[s, owner], g_send.at[turn, s, at], g_recv.at[turn, s, at], peer
+        ).start()
+
+    def gather_steps(turn, s, buf, use, forwarded=False):
+        def step(at, carry):
+            h = jnp.where(at < 2, 0, jnp.where(at <= n_line, at - 1, at - n_line))
+            other = jnp.where(at < 2, at, jnp.where(at <= n_line, 0, 1))
+            owner = lax.rem(line + n_line - h, n_line) * 2 + lax.rem(side + other, 2)
+
+            @pl.when((at == 1) | (at > n_line))
+            def _():
+                gather_wait(turn, s, buf, at, owner)
+
+            if not forwarded:
+
+                @pl.when((at >= 2) & (at <= n_line))
+                def _():
+                    gather_forward(turn, s, buf, h)
+
+            use(owner)
+            return carry
+
+        lax.fori_loop(0, n_mp, step, 0)
+
+    def each_stream(body):
+        def step(s, carry):
+            body(s)
+            return carry
+
+        lax.fori_loop(0, streams, step, 0)
+
+    def third_rows(own, gathered):
+        total = own_weight * own[seq_dev - 1].astype(F32)
+        for q in range(n_dp):
+            total = total + part_weight[q] * gathered[q].astype(F32)
+        return total
+
+    kept = (seq_dev - 1) * tokens
+    for b in range(seq_dev - 1):
+        noise_rows[pl.ds(b * tokens, tokens)] = noise_ref[b]
+    ready = kept // part_rows
+
+    def first_start(s):
+        u0[s, mp] = noise_rows[pl.ds(s * part_rows, part_rows)]
+        gather_start(0, s, u0)
+
+    for s in range(ready):
+        first_start(s)
+    noise_all[dp] = noise_ref[seq_dev]
+    for copy in in_copies[0]:
+        copy.wait_recv()
+    noise_rows[pl.ds(kept, tokens)] = third_rows(noise_ref, noise_all).astype(BF16)
+    for s in range(ready, streams):
+        first_start(s)
+    cross(1, prelude_ref, pre_all)
+    cross(2, cot_ref.at[seq_dev], cot_all)
+    pre_all[dp] = prelude_ref[...]
+    cot_all[dp] = cot_ref[seq_dev]
+
+    w_copy.wait()
+    waiting = [(s, h) for s in range(streams) for h in range(1, n_line)]
+    for k in range(n_mp):
+        w8[k] = w_ref[:, k * width : (k + 1) * width]
+        gain_ref[k] = gain_in[:, k * width : (k + 1) * width]
+        take = -(-len(waiting) // (n_mp - k))
+        for s, h in waiting[:take]:
+            gather_forward(0, s, u0, h)
+        waiting = waiting[take:]
+
+    for copy in in_copies[1]:
+        copy.wait_recv()
+    for b in range(seq_dev):
+
+        def add(q, t, b=b):
+            for i in range(seq_dev):
+                t = t + pick_ref[b * seqs + q * seq_dev + i] * pre_all[q, i].astype(F32)
+            return t
+
+        inject[pl.ds(b * tokens, tokens)] = lax.fori_loop(
+            0, n_dp, add, jnp.zeros((tokens, width), F32)
+        )
+
+    def rows_of(s):
+        return pl.ds(pl.multiple_of(s * part_rows, part_rows), part_rows)
+
+    def active(turn, s):
+        return counts_ref[rows_of(s)] >= float(MAXR - turn)
+
+    def first(s):
+        acc[s] = jnp.zeros((part_rows, width), F32)
+
+        def use(k):
+            acc[s] += lax.dot_general(u0[s, k], w8[k], NT, preferred_element_type=F32)
+
+        gather_steps(0, s, u0, use, forwarded=True)
+        y0[s, mp] = (acc[s] + inject[rows_of(s)]).astype(BF16)
+        gather_start(1, s, y0)
+
+    each_stream(first)
+
+    def renew(turn, s, y_all, before, after):
+        live = active(turn, s)
+        acc[s] = jnp.zeros((part_rows, width), F32)
+        square[...] = jnp.zeros_like(square)
+
+        def use(k):
+            y = y_all[s, k].astype(F32)
+            square[...] += jnp.sum(y * y, axis=1, keepdims=True)
+            new = jnp.where(live, gain_ref[k] * y, before[s, k].astype(F32)).astype(BF16)
+            after[s, k] = new
+            acc[s] += lax.dot_general(new, w8[k], NT, preferred_element_type=F32)
+            to = k // blocks
+            part = lax.rem(k, blocks)
+            dst = xs.at[part, turn, s, dp]
+
+            @pl.when(to == dp)
+            def _():
+                pltpu.make_async_copy(after.at[s, k], dst, own_sem.at[turn, s, part]).start()
+
+            @pl.when(to != dp)
+            def _():
+                remote(
+                    after.at[s, k], dst, x_send.at[turn, s, k], x_recv.at[turn, s, dp, part],
+                    (to, mp),
+                ).start()
+
+        gather_steps(1 + turn, s, y_all, use)
+        root = lax.rsqrt(square[...] / full_width + EPS)
+        rms[turn, rows_of(s)] = root
+        previous = 1.0 if turn == 0 else scale[turn - 1, rows_of(s)]
+        scale[turn, rows_of(s)] = jnp.where(live, root, previous)
+
+    def second(s):
+        renew(0, s, y0, u0, u1)
+        y1[s, mp] = (scale[0, rows_of(s)] * acc[s] + inject[rows_of(s)]).astype(BF16)
+        gather_start(2, s, y1)
+
+    each_stream(second)
+
+    for copy in in_copies[2]:
+        copy.wait_recv()
+    gain = gain_ref[mp]
+    cot_rows[pl.ds(kept, tokens)] = third_rows(cot_ref, cot_all)
+    for b in range(seq_dev - 1):
+        cot_rows[pl.ds(b * tokens, tokens)] = cot_ref[b].astype(F32)
+    scaled[...] = cot_rows[...] * gain
+
+    def sums_start(which, s, values):
+        ones = jnp.ones((4, width), F32)
+        lines = [
+            lax.dot_general(
+                ones, v, NT, preferred_element_type=F32, precision=lax.Precision.HIGHEST
+            )
+            for v in values
+        ]
+        red[which, s, mp] = jnp.concatenate(lines, axis=0)
+        own = red.at[which, s, mp]
+        for o in range(1, n_mp):
+            remote(
+                own, own, red_send.at[which, s, o], red_recv.at[which, s, o],
+                (dp, lax.rem(mp + o, n_mp)),
+            ).start()
+
+    def sums_end(which, s):
+        own = red.at[which, s, mp]
+        for o in range(1, n_mp):
+            remote(
+                own, own, red_send.at[which, s, o], red_recv.at[which, s, o], peer
+            ).wait_recv()
+        total = red[which, s, 0]
+        for k in range(1, n_mp):
+            total = total + red[which, s, k]
+        columns = jnp.transpose(total)
+        return columns[:, 0:1], columns[:, 4:5]
+
+    def third(s):
+        renew(1, s, y1, u1, u2)
+        y = (scale[1, rows_of(s)] * acc[s] + inject[rows_of(s)]).astype(BF16).astype(F32)
+        y_last[rows_of(s)] = y
+        sums_start(0, s, (y * y, scaled[rows_of(s)] * y))
+
+    each_stream(third)
+
+    dp_pair, dp_side = dp // 2, lax.rem(dp, 2)
+    n_pair = n_dp // 2
+    dp_peer = (dp_pair * 2 + 1 - dp_side, mp)
+
+    def spread_copies(which, s):
+        own, dst = spread_own.at[which, s], ds.at[which, s, dp]
+        copies = []
+        for h in range(1, n_pair):
+            to = (lax.rem(dp_pair + h, n_pair) * 2 + dp_side, mp)
+            copies.append(remote(own, dst, d_send.at[which, s, h], d_recv.at[which, s, h], to))
+        copies.append(remote(own, dst, d_send.at[which, s, 0], d_recv.at[which, s, 0], dp_peer))
+        return copies, pltpu.make_async_copy(own, dst, own_sem.at[which, s, blocks])
+
+    def spread_start(which, s, values):
+        spread_own[which, s] = values
+        copies, local_copy = spread_copies(which, s)
+        for copy in copies:
+            copy.start()
+        local_copy.start()
+
+    def spread_forwards(which, s):
+        forwards = []
+        for h in range(1, n_pair):
+            held = ds.at[which, s, lax.rem(dp_pair + n_pair - h, n_pair) * 2 + dp_side]
+            f = n_pair + h
+            forwards.append(
+                remote(held, held, d_send.at[which, s, f], d_recv.at[which, s, f], dp_peer)
+            )
+        return forwards
+
+    def spread_forward(which, s):
+        copies, unused = spread_copies(which, s)
+        for copy, forward in zip(copies, spread_forwards(which, s)):
+            copy.wait_recv()
+            forward.start()
+
+    def pair_copy(s, at):
+        return remote(
+            pair_send.at[s, at], pair_recv.at[s, at], p_send.at[s, at], p_recv.at[s, at], peer
+        )
+
+    def line_copy(s, at):
+        to = (dp, lax.rem(line + at + 1, n_line) * 2 + side)
+        return remote(
+            line_send.at[s, at], line_recv.at[s, at], l_send.at[s, at], l_recv.at[s, at], to
+        )
+
+    def back_first(s):
+        square2, inner2 = sums_end(0, s)
+        root = lax.rsqrt(square2 / full_width + EPS)
+        y = y_last[rows_of(s)]
+        delta = jnp.where(
+            active(2, s),
+            root * scaled[rows_of(s)] - y * (root * root * root * inner2 / full_width),
+            0.0,
+        )
+        delta_b[s] = delta.astype(BF16)
+
+        def pair_step(at, carry):
+            to_line = lax.rem(line + at + 1, n_line)
+            product = jnp.dot(
+                delta_b[s], w8[to_line * 2 + 1 - side], preferred_element_type=F32
+            )
+            pair_send[s, at] = product.astype(BF16)
+            pair_copy(s, at).start()
+            return carry
+
+        lax.fori_loop(0, n_line, pair_step, 0)
+        spread_start(1, s, (delta * scale[1, rows_of(s)]).astype(BF16))
+        inner = delta_b[s].astype(F32) * acc[s]
+        sums_start(1, s, (inner, inner))
+
+    each_stream(back_first)
+
+    def back_second(s):
+        def line_step(at, carry):
+            to_line = lax.rem(line + at + 1, n_line)
+            product = jnp.dot(delta_b[s], w8[to_line * 2 + side], preferred_element_type=F32)
+            pair_copy(s, at).wait_recv()
+            total = product.astype(BF16).astype(F32) + pair_recv[s, at].astype(F32)
+            total_ref[s] = total
+
+            @pl.when(at < n_line - 1)
+            def _():
+                line_send[s, at] = total.astype(BF16)
+                line_copy(s, at).start()
+
+            return carry
+
+        lax.fori_loop(0, n_line, line_step, 0)
+
+    each_stream(back_second)
+    for s in range(streams):
+        spread_forward(1, s)
+
+    def back_third(s):
+        unused, inner = sums_end(1, s)
+        total = total_ref[s]
+        for at in range(n_line - 1):
+            line_copy(s, at).wait_recv()
+            total = total + line_recv[s, at].astype(F32)
+        upstream = jnp.where(active(2, s), total, cot_rows[rows_of(s)])
+        y = y1[s, mp].astype(F32)
+        root = rms[1, rows_of(s)]
+        delta = jnp.where(
+            active(1, s),
+            root * (upstream * gain) - y * (root * root * root * inner / full_width),
+            0.0,
+        )
+        spread_start(0, s, (delta * scale[0, rows_of(s)]).astype(BF16))
+
+    each_stream(back_third)
+    for s in range(streams):
+        spread_forward(0, s)
+
+    def finish(s):
+        for which in range(BP):
+            copies, local_copy = spread_copies(which, s)
+            copies[-1].wait_recv()
+            for copy in spread_forwards(which, s):
+                copy.wait()
+            for copy in copies:
+                copy.wait_send()
+            local_copy.wait()
+            for part in range(blocks):
+                pltpu.make_async_copy(
+                    u1.at[s, 0], xs.at[part, which, s, dp], own_sem.at[which, s, part]
+                ).wait()
+                for h in range(1, n_dp):
+                    q = lax.rem(dp + h, n_dp)
+                    copy = remote(
+                        u1.at[s, 0], xs.at[part, which, s, q],
+                        x_send.at[which, s, q * blocks + part], x_recv.at[which, s, q, part],
+                        (q, mp),
+                    )
+                    copy.wait()
+            own = red.at[which, s, mp]
+            for o in range(1, n_mp):
+                remote(
+                    own, own, red_send.at[which, s, o], red_recv.at[which, s, o], peer
+                ).wait_send()
+        for turn, buf in enumerate((u0, y0, y1)):
+            for at in range(1, n_mp):
+                remote(
+                    buf.at[s, mp], buf.at[s, mp], g_send.at[turn, s, at], g_recv.at[turn, s, at],
+                    peer,
+                ).wait_send()
+        for at in range(n_line):
+            pair_copy(s, at).wait_send()
+        for at in range(n_line - 1):
+            line_copy(s, at).wait_send()
+
+    each_stream(finish)
+    for copies in in_copies:
+        for copy in copies:
+            copy.wait_send()
+
+
+def grad_kernel(ds_ref, xs_ref, out_ref):
+    width = ds_ref.shape[-1]
+    left = ds_ref[...].reshape(-1, width)
+    depth = left.shape[0]
+    full = xs_ref.shape[-1]
+    for part in range(xs_ref.shape[0]):
+        right = xs_ref[part].reshape(depth, full)
+        out_ref[:, part * full : (part + 1) * full] = lax.dot_general(
+            left, right, TN, preferred_element_type=F32
+        )
+
+
+def fused(
+    n_dp, n_mp, streams,
+    prelude_output, init_noise, core_weight, norm_gain, state_cotangent, step_counts, group_table,
+):
+    width, full_width = core_weight.shape
+    seq_dev, tokens = prelude_output.shape[:2]
+    cap = init_noise.shape[0]
+    seqs = group_table.shape[0]
+    rows = seq_dev * tokens
+    part_rows = rows // streams
+    blocks = n_mp // n_dp
+    n_line, n_pair = n_mp // 2, n_dp // 2
+    vmem = pl.BlockSpec(memory_space=pltpu.VMEM)
+    smem = pl.BlockSpec(memory_space=pltpu.SMEM)
+    any_space = pl.BlockSpec(memory_space=pl.ANY)
+    state = pltpu.VMEM((streams, n_mp, part_rows, width), BF16)
+    row_f32 = pltpu.VMEM((rows, width), F32)
+    stream_f32 = pltpu.VMEM((streams, part_rows, width), F32)
+    pieces = pltpu.VMEM((streams, n_line, part_rows, width), BF16)
+    dma = pltpu.SemaphoreType.DMA
+    scratch = [
+        pltpu.VMEM((width, full_width), BF16),
+        pltpu.VMEM((n_mp, width, width), BF16),
+        state, state, state, state, state,
+        pltpu.VMEM((n_mp, 1, width), F32),
+        pltpu.VMEM((rows, 1), F32),
+        pltpu.SMEM((seq_dev * seqs,), F32),
+        row_f32, stream_f32,
+        pltpu.VMEM((part_rows, 1), F32),
+        pltpu.VMEM((BP, rows, 1), F32),
+        pltpu.VMEM((BP, rows, 1), F32),
+        row_f32, row_f32, row_f32,
+        pltpu.VMEM((streams, part_rows, width), BF16),
+        pltpu.VMEM((BP, streams, part_rows, width), BF16),
+        stream_f32,
+        pltpu.VMEM((rows, width), BF16),
+        pltpu.VMEM((n_dp, seq_dev, tokens, width), BF16),
+        pltpu.VMEM((n_dp, tokens, width), BF16),
+        pltpu.VMEM((n_dp, tokens, width), BF16),
+        pltpu.VMEM((BP, streams, n_mp, 8, part_rows), F32),
+        pieces, pieces, pieces, pieces,
+        dma,
+        dma((3, n_dp)), dma((3, n_dp)),
+        dma((MAXR, streams, n_mp)), dma((MAXR, streams, n_mp)),
+        dma((BP, streams, n_mp)), dma((BP, streams, n_dp, blocks)),
+        dma((BP, streams, blocks + 1)),
+        dma((BP, streams, 2 * n_pair)), dma((BP, streams, 2 * n_pair)),
+        dma((BP, streams, n_mp)), dma((BP, streams, n_mp)),
+        dma((streams, n_line)), dma((streams, n_line)),
+        dma((streams, n_line)), dma((streams, n_line)),
+    ]
+    deltas, states = pl.pallas_call(
+        functools.partial(core_kernel, n_dp, n_mp, streams, full_width, cap),
+        out_shape=(
+            jax.ShapeDtypeStruct((BP, streams, n_dp, part_rows, width), BF16),
+            jax.ShapeDtypeStruct((blocks, BP, streams, n_dp, part_rows, width), BF16),
+        ),
+        in_specs=[smem] * 2 + [vmem] * 4 + [any_space],
+        out_specs=(any_space, any_space),
+        scratch_shapes=scratch,
+        compiler_params=pltpu.CompilerParams(
+            collective_id=0, has_side_effects=True, vmem_limit_bytes=56 * 1024 * 1024
+        ),
+        cost_estimate=pl.CostEstimate(
+            flops=2 * rows * full_width * width * 4, bytes_accessed=20_000_000, transcendentals=0
+        ),
+    )(
+        step_counts, group_table, prelude_output, init_noise, state_cotangent,
+        norm_gain.reshape(1, full_width), core_weight,
+    )
+    tile = 256
+    return pl.pallas_call(
+        grad_kernel,
+        grid=(pl.cdiv(width, tile),),
+        out_shape=jax.ShapeDtypeStruct((width, blocks * width), F32),
+        in_specs=[
+            pl.BlockSpec((BP, streams, n_dp, part_rows, tile), lambda i: (0, 0, 0, 0, i)),
+            pl.BlockSpec(states.shape, lambda i: (0,) * 6),
+        ],
+        out_specs=pl.BlockSpec((tile, blocks * width), lambda i: (i, 0)),
+        compiler_params=pltpu.CompilerParams(vmem_limit_bytes=48 * 1024 * 1024),
+    )(deltas, states)
+
+
 def solution(mesh):
+    n_dp, n_mp = mesh.shape["dp"], mesh.shape["mp"]
+    paired = n_mp % n_dp == 0 and n_mp % 2 == 0 and n_dp % 2 == 0
     return jax.shard_map(
-        local,
+        functools.partial(fused, n_dp, n_mp, STREAMS) if paired else local,
         mesh=mesh,
         in_specs=(
             P("dp", None, "mp"),

time: 357 us -> 99.6 us (0.28)
  waiting for transfers between devices: 182 us -> 0 us
  Pallas kernels: 0 us -> 94.8 us
  blocking collectives: 77.4 us -> 0 us
  matrix products: 39.2 us -> 0 us
  local copies, waits for them, and re-layouts: 26.7 us -> 4.29 us
  other arithmetic: 15.4 us -> 0 us
  between operations: 14.1 us -> 0.02 us
    all_gather x3 -> x0, waiting for transfers between devices: 113 us -> none  [the longest x2 78.3 us: local(): lax.all_gather(mixed, 'mp', axis=1, tiled=True).astype(jnp.float32)]
    pallas_call x0 -> x2, Pallas kernels: none -> 94.8 us  [the longest x1 90.9 us: fused(): pl.pallas_call(functools.partial(core_kernel, n_dp, n_mp, streams, full_w...]
    unnamed x6 -> x0, waiting for transfers between devices: 68.8 us -> none
    dot_general x7 -> x0, matrix products: 39.2 us -> none  [the longest x2 17.1 us: local(): lax.dot_general(delta_b, whole_state, (((0,), (0,)), ((), ())), preferred...]
    psum x2 -> x0, blocking collectives: 37.4 us -> none  [feature_sum(): return lax.psum(values, 'mp')]
    unnamed x1 -> x0, blocking collectives: 30.9 us -> none
    unnamed x39 -> x4, local copies, waits for them, and re-layouts: 20.5 us -> 2.93 us
    all_gather x1 -> x0, blocking collectives: 9.18 us -> none  [local(): lax.all_gather(prelude_output, 'dp', axis=0, tiled=True)]
  transfers between devices with their start and end apart: 5 -> 0, of which waited for: 4 -> 0; matrix products, arithmetic and copies ran while one was open for 4% -> 0% of each run, Pallas kernels for 0% -> 0%
where the time goes in v2:
time: 99.6 us; the launch traced here: 99.1 us
  Pallas kernels  94.8 us (95%)
  local copies, waits for them, and re-layouts  4.29 us (4%)
    pallas_call x1, Pallas kernels, fused(): pl.pallas_call(functools.partial(core_kernel, n_dp, n_mp, streams, full_w...  90.9 us
    pallas_call x1, Pallas kernels, fused(): pl.pallas_call(grad_kernel, grid=(pl.cdiv(width, tile),), out_shape=jax.S...  3.96 us
    unnamed x4, local copies, waits for them, and re-layouts  2.93 us

profile of v2, /device:TPU:0, one launch (start us, length us, event | category | flops | bytes accessed | tf_op | source)
XLA Modules:
  0.0 99.1 jit_solution(12355001786620755838)
XLA Ops:
  0.0 1.4 %reshape.3.gain_in = f32[1,5280]{1,0:T(1,128)} reshape(f32[5280]{0:T(1024)} %param.10) | data formatting | bytes 42240 | tf_op jit(solution)/shard_map/reshape | solution.py:650
  1.4 90.9 %shard_map.73 = (bf16[2,2,4,48,660]{4,3,2,1,0:T(8,128)(2,1)}, bf16[2,2,2,4,48,660]{5,4,3,2,1,0:T(8,128)(2,1)}) custom-call(s32[12]{0:T(128)} %counts_in.1, s32[12]{0:T(128)} %groups_in.1, bf16[3,32,660]{2,1,0:T(8,128)(2,1)} %prelude_ref.1, bf16[4,32,660]{2,1,0:T(8,128)(2,1)} %noise_ref.1, bf16[4,32,660]{2,1,0:T(8,128)(2,1)} %cot_ref.1, ...), custom_call_target="tpu_custom_call" | custom-call | flops 2676326400 | bytes 20000000 | tf_op jit(solution)/shard_map/pallas_call | solution.py:633
  92.2 0.0 copy-start
  92.2 1.7 %copy-done = bf16[2,2,2,4,48,660]{5,4,3,2,1,0:T(8,128)(2,1)S(1)} copy-done((bf16[2,2,2,4,48,660]{5,4,3,2,1,0:T(8,128)(2,1)S(1)}, bf16[2,2,2,4,48,660]{5,4,3,2,1,0:T(8,128)(2,1)}, u32[]{:S(2)}) %copy-start) | copy-done | bytes 2027544
  93.9 0.0 copy-start.1
  93.9 1.3 %copy-done.1 = bf16[2,2,4,48,660]{4,3,2,1,0:T(8,128)(2,1)S(1)} copy-done((bf16[2,2,4,48,660]{4,3,2,1,0:T(8,128)(2,1)S(1)}, bf16[2,2,4,48,660]{4,3,2,1,0:T(8,128)(2,1)}, u32[]{:S(2)}) %copy-start.1) | copy-done | bytes 1013784
  95.2 4.0 %shard_map.74 = f32[660,1320]{1,0:T(8,128)} custom-call(bf16[2,2,4,48,660]{4,3,2,1,0:T(8,128)(2,1)S(1)} %copy-done.1, bf16[2,2,2,4,48,660]{5,4,3,2,1,0:T(8,128)(2,1)S(1)} %copy-done), custom_call_target="tpu_custom_call" | custom-call | tf_op jit(solution)/shard_map/pallas_call | solution.py:653
Async XLA Ops:
  92.2 1.7 %copy-start = (bf16[2,2,2,4,48,660]{5,4,3,2,1,0:T(8,128)(2,1)S(1)}, bf16[2,2,2,4,48,660]{5,4,3,2,1,0:T(8,128)(2,1)}, u32[]{:S(2)}) copy-start(bf16[2,2,2,4,48,660]{5,4,3,2,1,0:T(8,128)(2,1)} %get-tuple-element.8.xs_ref) | copy-start | bytes 6082564
  93.9 1.3 %copy-start.1 = (bf16[2,2,4,48,660]{4,3,2,1,0:T(8,128)(2,1)S(1)}, bf16[2,2,4,48,660]{4,3,2,1,0:T(8,128)(2,1)}, u32[]{:S(2)}) copy-start(bf16[2,2,4,48,660]{4,3,2,1,0:T(8,128)(2,1)} %get-tuple-element.7.ds_ref) | copy-start | bytes 3041284

commit v3 on v2

--- a/solution.py
+++ b/solution.py
@@ -10,7 +10,7 @@
 MESH = pl.DeviceIdType.MESH
 NT = (((1,), (1,)), ((), ()))
 TN = (((0,), (0,)), ((), ()))
-STREAMS = 2
+STREAMS = 3
 F32 = jnp.float32
 BF16 = jnp.bfloat16
 MAXR = 3
@@ -289,7 +289,7 @@
     waiting = [(s, h) for s in range(streams) for h in range(1, n_line)]
     for k in range(n_mp):
         w8[k] = w_ref[:, k * width : (k + 1) * width]
-        gain_ref[k] = gain_in[:, k * width : (k + 1) * width]
+        gain_ref[k] = gain_in[pl.ds(k * width, width)].reshape(1, width)
         take = -(-len(waiting) // (n_mp - k))
         for s, h in waiting[:take]:
             gather_forward(0, s, u0, h)
@@ -381,7 +381,7 @@
             )
             for v in values
         ]
-        red[which, s, mp] = jnp.concatenate(lines, axis=0)
+        red[which, s, mp] = jnp.concatenate(lines * (2 // len(lines)), axis=0)
         own = red.at[which, s, mp]
         for o in range(1, n_mp):
             remote(
@@ -479,7 +479,7 @@
         lax.fori_loop(0, n_line, pair_step, 0)
         spread_start(1, s, (delta * scale[1, rows_of(s)]).astype(BF16))
         inner = delta_b[s].astype(F32) * acc[s]
-        sums_start(1, s, (inner, inner))
+        sums_start(1, s, (inner,))
 
     each_stream(back_first)
 
@@ -647,7 +647,7 @@
         ),
     )(
         step_counts, group_table, prelude_output, init_noise, state_cotangent,
-        norm_gain.reshape(1, full_width), core_weight,
+        norm_gain, core_weight,
     )
     tile = 256
     return pl.pallas_call(
@@ -659,7 +659,7 @@
             pl.BlockSpec(states.shape, lambda i: (0,) * 6),
         ],
         out_specs=pl.BlockSpec((tile, blocks * width), lambda i: (i, 0)),
-        compiler_params=pltpu.CompilerParams(vmem_limit_bytes=48 * 1024 * 1024),
+        compiler_params=pltpu.CompilerParams(vmem_limit_bytes=60 * 1024 * 1024),
     )(deltas, states)
 
 

time: 99.6 us -> 104 us (1.044)
  Pallas kernels: 94.8 us -> 103 us
  local copies, waits for them, and re-layouts: 4.29 us -> 0 us
    pallas_call x1, Pallas kernels: 90.9 us -> 97.4 us  [fused(): pl.pallas_call(functools.partial(core_kernel, n_dp, n_mp, streams, full_w...]
    unnamed x4 -> x0, local copies, waits for them, and re-layouts: 2.93 us -> none
    pallas_call x1, Pallas kernels: 3.96 us -> 5.94 us  [fused(): pl.pallas_call(grad_kernel, grid=(pl.cdiv(width, tile),), out_shape=jax.S...]
    reshape x1 -> x0, local copies, waits for them, and re-layouts: 1.36 us -> none  [fused(): norm_gain.reshape(1, full_width)]
where the time goes in v3:
time: 104 us; the launch traced here: 103 us
  Pallas kernels  103 us (99%)
    pallas_call x1, Pallas kernels, fused(): pl.pallas_call(functools.partial(core_kernel, n_dp, n_mp, streams, full_w...  97.4 us
    pallas_call x1, Pallas kernels, fused(): pl.pallas_call(grad_kernel, grid=(pl.cdiv(width, tile),), out_shape=jax.S...  5.94 us

profile of v3, /device:TPU:0, one launch (start us, length us, event | category | flops | bytes accessed | tf_op | source)
XLA Modules:
  0.0 103.3 jit_solution(3050283776690167353)
XLA Ops:
  0.0 97.4 %shard_map.73 = (bf16[2,3,4,32,660]{4,3,2,1,0:T(8,128)(2,1)}, bf16[2,2,3,4,32,660]{5,4,3,2,1,0:T(8,128)(2,1)}) custom-call(s32[12]{0:T(128)} %counts_in.1, s32[12]{0:T(128)} %groups_in.1, bf16[3,32,660]{2,1,0:T(8,128)(2,1)} %prelude_ref.1, bf16[4,32,660]{2,1,0:T(8,128)(2,1)} %noise_ref.1, bf16[4,32,660]{2,1,0:T(8,128)(2,1)} %cot_ref.1, f32[5280]{0:T(1024)} %gain_in.1, ...), custom_call_target="tpu_custom_call" | custom-call | flops 2676326400 | bytes 20000000 | tf_op jit(solution)/shard_map/pallas_call | solution.py:633
  97.4 5.9 %shard_map.74 = f32[660,1320]{1,0:T(8,128)} custom-call(bf16[2,3,4,32,660]{4,3,2,1,0:T(8,128)(2,1)} %get-tuple-element.7.ds_ref, bf16[2,2,3,4,32,660]{5,4,3,2,1,0:T(8,128)(2,1)} %get-tuple-element.8.xs_ref), custom_call_target="tpu_custom_call" | custom-call | tf_op jit(solution)/shard_map/pallas_call | solution.py:653

commit v4 on v3

--- a/solution.py
+++ b/solution.py
@@ -10,7 +10,7 @@
 MESH = pl.DeviceIdType.MESH
 NT = (((1,), (1,)), ((), ()))
 TN = (((0,), (0,)), ((), ()))
-STREAMS = 3
+STREAMS = 2
 F32 = jnp.float32
 BF16 = jnp.bfloat16
 MAXR = 3
@@ -266,34 +266,31 @@
     kept = (seq_dev - 1) * tokens
     for b in range(seq_dev - 1):
         noise_rows[pl.ds(b * tokens, tokens)] = noise_ref[b]
-    ready = kept // part_rows
 
     def first_start(s):
         u0[s, mp] = noise_rows[pl.ds(s * part_rows, part_rows)]
         gather_start(0, s, u0)
 
-    for s in range(ready):
-        first_start(s)
+    first_start(0)
     noise_all[dp] = noise_ref[seq_dev]
     for copy in in_copies[0]:
         copy.wait_recv()
     noise_rows[pl.ds(kept, tokens)] = third_rows(noise_ref, noise_all).astype(BF16)
-    for s in range(ready, streams):
-        first_start(s)
     cross(1, prelude_ref, pre_all)
     cross(2, cot_ref.at[seq_dev], cot_all)
     pre_all[dp] = prelude_ref[...]
     cot_all[dp] = cot_ref[seq_dev]
 
     w_copy.wait()
-    waiting = [(s, h) for s in range(streams) for h in range(1, n_line)]
+    waiting = list(range(1, n_line))
     for k in range(n_mp):
         w8[k] = w_ref[:, k * width : (k + 1) * width]
         gain_ref[k] = gain_in[pl.ds(k * width, width)].reshape(1, width)
-        take = -(-len(waiting) // (n_mp - k))
-        for s, h in waiting[:take]:
-            gather_forward(0, s, u0, h)
-        waiting = waiting[take:]
+        if k >= 1 and waiting:
+            gather_forward(0, 0, u0, waiting.pop(0))
+            if not waiting:
+                for s in range(1, streams):
+                    first_start(s)
 
     for copy in in_copies[1]:
         copy.wait_recv()
@@ -314,17 +311,18 @@
     def active(turn, s):
         return counts_ref[rows_of(s)] >= float(MAXR - turn)
 
-    def first(s):
+    def first(s, forwarded):
         acc[s] = jnp.zeros((part_rows, width), F32)
 
         def use(k):
             acc[s] += lax.dot_general(u0[s, k], w8[k], NT, preferred_element_type=F32)
 
-        gather_steps(0, s, u0, use, forwarded=True)
+        gather_steps(0, s, u0, use, forwarded=forwarded)
         y0[s, mp] = (acc[s] + inject[rows_of(s)]).astype(BF16)
         gather_start(1, s, y0)
 
-    each_stream(first)
+    for s in range(streams):
+        first(s, s == 0)
 
     def renew(turn, s, y_all, before, after):
         live = active(turn, s)

time: 104 us -> 97.1 us (0.934)
  Pallas kernels: 103 us -> 96.9 us
    pallas_call x1, Pallas kernels: 97.4 us -> 91 us  [fused(): pl.pallas_call(functools.partial(core_kernel, n_dp, n_mp, streams, full_w...]
where the time goes in v4:
time: 97.1 us; the launch traced here: 96.9 us
  Pallas kernels  96.9 us (100%)
    pallas_call x1, Pallas kernels, fused(): pl.pallas_call(functools.partial(core_kernel, n_dp, n_mp, streams, full_w...  91 us
    pallas_call x1, Pallas kernels, fused(): pl.pallas_call(grad_kernel, grid=(pl.cdiv(width, tile),), out_shape=jax.S...  5.94 us

profile of v4, /device:TPU:0, one launch (start us, length us, event | category | flops | bytes accessed | tf_op | source)
XLA Modules:
  0.0 96.9 jit_solution(15828098907093696269)
XLA Ops:
  0.0 91.0 %shard_map.73 = (bf16[2,2,4,48,660]{4,3,2,1,0:T(8,128)(2,1)}, bf16[2,2,2,4,48,660]{5,4,3,2,1,0:T(8,128)(2,1)}) custom-call(s32[12]{0:T(128)} %counts_in.1, s32[12]{0:T(128)} %groups_in.1, bf16[3,32,660]{2,1,0:T(8,128)(2,1)} %prelude_ref.1, bf16[4,32,660]{2,1,0:T(8,128)(2,1)} %noise_ref.1, bf16[4,32,660]{2,1,0:T(8,128)(2,1)} %cot_ref.1, f32[5280]{0:T(1024)} %gain_in.1, ...), custom_call_target="tpu_custom_call" | custom-call | flops 2676326400 | bytes 20000000 | tf_op jit(solution)/shard_map/pallas_call | solution.py:631
  91.0 5.9 %shard_map.74 = f32[660,1320]{1,0:T(8,128)} custom-call(bf16[2,2,4,48,660]{4,3,2,1,0:T(8,128)(2,1)} %get-tuple-element.7.ds_ref, bf16[2,2,2,4,48,660]{5,4,3,2,1,0:T(8,128)(2,1)} %get-tuple-element.8.xs_ref), custom_call_target="tpu_custom_call" | custom-call | tf_op jit(solution)/shard_map/pallas_call | solution.py:651

commit v5 on v4

--- a/solution.py
+++ b/solution.py
@@ -105,6 +105,46 @@
     return lax.psum_scatter(
         weight_grad.astype(jnp.bfloat16), "dp", scatter_dimension=1, tiled=True
     ).astype(jnp.float32)
+
+
+LANES = 128
+GROUP = 16
+
+
+def packed_rows(part_rows, width):
+    rest = width % LANES
+    if part_rows % GROUP or rest * (part_rows // GROUP) > LANES:
+        return None
+    return width // LANES * part_rows + (GROUP if rest else 0)
+
+
+def pack(ref, values):
+    part_rows, width = values.shape
+    whole = width // LANES
+    rest = width - whole * LANES
+    for c in range(whole):
+        ref[pl.ds(c * part_rows, part_rows)] = values[:, c * LANES : (c + 1) * LANES].astype(BF16)
+    if rest:
+        groups = part_rows // GROUP
+        pieces = [
+            values[g * GROUP : (g + 1) * GROUP, whole * LANES :].astype(F32) for g in range(groups)
+        ]
+        pieces.append(jnp.zeros((GROUP, LANES - groups * rest), F32))
+        ref[pl.ds(whole * part_rows, GROUP)] = jnp.concatenate(pieces, axis=1).astype(BF16)
+
+
+def unpack(ref, part_rows, width):
+    whole = width // LANES
+    rest = width - whole * LANES
+    columns = [ref[pl.ds(c * part_rows, part_rows)].astype(F32) for c in range(whole)]
+    if rest:
+        last = ref[pl.ds(whole * part_rows, GROUP)].astype(F32)
+        columns.append(
+            jnp.concatenate(
+                [last[:, g * rest : (g + 1) * rest] for g in range(part_rows // GROUP)], axis=0
+            )
+        )
+    return jnp.concatenate(columns, axis=1)
 
 
 def core_kernel(
@@ -268,7 +308,7 @@
         noise_rows[pl.ds(b * tokens, tokens)] = noise_ref[b]
 
     def first_start(s):
-        u0[s, mp] = noise_rows[pl.ds(s * part_rows, part_rows)]
+        pack(u0.at[s, mp], noise_rows[pl.ds(s * part_rows, part_rows)])
         gather_start(0, s, u0)
 
     first_start(0)
@@ -315,24 +355,25 @@
         acc[s] = jnp.zeros((part_rows, width), F32)
 
         def use(k):
-            acc[s] += lax.dot_general(u0[s, k], w8[k], NT, preferred_element_type=F32)
+            acc[s] += lax.dot_general(
+                unpack(u0.at[s, k], part_rows, width).astype(BF16), w8[k], NT, preferred_element_type=F32)
 
         gather_steps(0, s, u0, use, forwarded=forwarded)
-        y0[s, mp] = (acc[s] + inject[rows_of(s)]).astype(BF16)
+        pack(y0.at[s, mp], acc[s] + inject[rows_of(s)])
         gather_start(1, s, y0)
 
     for s in range(streams):
         first(s, s == 0)
 
-    def renew(turn, s, y_all, before, after):
+    def renew(turn, s, y_all, old_block, after):
         live = active(turn, s)
         acc[s] = jnp.zeros((part_rows, width), F32)
         square[...] = jnp.zeros_like(square)
 
         def use(k):
-            y = y_all[s, k].astype(F32)
+            y = unpack(y_all.at[s, k], part_rows, width)
             square[...] += jnp.sum(y * y, axis=1, keepdims=True)
-            new = jnp.where(live, gain_ref[k] * y, before[s, k].astype(F32)).astype(BF16)
+            new = jnp.where(live, gain_ref[k] * y, old_block(k)).astype(BF16)
             after[s, k] = new
             acc[s] += lax.dot_general(new, w8[k], NT, preferred_element_type=F32)
             to = k // blocks
@@ -357,8 +398,8 @@
         scale[turn, rows_of(s)] = jnp.where(live, root, previous)
 
     def second(s):
-        renew(0, s, y0, u0, u1)
-        y1[s, mp] = (scale[0, rows_of(s)] * acc[s] + inject[rows_of(s)]).astype(BF16)
+        renew(0, s, y0, lambda k: unpack(u0.at[s, k], part_rows, width), u1)
+        pack(y1.at[s, mp], scale[0, rows_of(s)] * acc[s] + inject[rows_of(s)])
         gather_start(2, s, y1)
 
     each_stream(second)
@@ -400,7 +441,7 @@
         return columns[:, 0:1], columns[:, 4:5]
 
     def third(s):
-        renew(1, s, y1, u1, u2)
+        renew(1, s, y1, lambda k: u1[s, k].astype(F32), u2)
         y = (scale[1, rows_of(s)] * acc[s] + inject[rows_of(s)]).astype(BF16).astype(F32)
         y_last[rows_of(s)] = y
         sums_start(0, s, (y * y, scaled[rows_of(s)] * y))
@@ -470,7 +511,7 @@
             product = jnp.dot(
                 delta_b[s], w8[to_line * 2 + 1 - side], preferred_element_type=F32
             )
-            pair_send[s, at] = product.astype(BF16)
+            pack(pair_send.at[s, at], product)
             pair_copy(s, at).start()
             return carry
 
@@ -486,12 +527,12 @@
             to_line = lax.rem(line + at + 1, n_line)
             product = jnp.dot(delta_b[s], w8[to_line * 2 + side], preferred_element_type=F32)
             pair_copy(s, at).wait_recv()
-            total = product.astype(BF16).astype(F32) + pair_recv[s, at].astype(F32)
+            total = product.astype(BF16).astype(F32) + unpack(pair_recv.at[s, at], part_rows, width)
             total_ref[s] = total
 
             @pl.when(at < n_line - 1)
             def _():
-                line_send[s, at] = total.astype(BF16)
+                pack(line_send.at[s, at], total)
                 line_copy(s, at).start()
 
             return carry
@@ -507,9 +548,9 @@
         total = total_ref[s]
         for at in range(n_line - 1):
             line_copy(s, at).wait_recv()
-            total = total + line_recv[s, at].astype(F32)
+            total = total + unpack(line_recv.at[s, at], part_rows, width)
         upstream = jnp.where(active(2, s), total, cot_rows[rows_of(s)])
-        y = y1[s, mp].astype(F32)
+        y = unpack(y1.at[s, mp], part_rows, width)
         root = rms[1, rows_of(s)]
         delta = jnp.where(
             active(1, s),
@@ -595,12 +636,14 @@
     state = pltpu.VMEM((streams, n_mp, part_rows, width), BF16)
     row_f32 = pltpu.VMEM((rows, width), F32)
     stream_f32 = pltpu.VMEM((streams, part_rows, width), F32)
-    pieces = pltpu.VMEM((streams, n_line, part_rows, width), BF16)
+    packed = packed_rows(part_rows, width)
+    travel = pltpu.VMEM((streams, n_mp, packed, LANES), BF16)
+    pieces = pltpu.VMEM((streams, n_line, packed, LANES), BF16)
     dma = pltpu.SemaphoreType.DMA
     scratch = [
         pltpu.VMEM((width, full_width), BF16),
         pltpu.VMEM((n_mp, width, width), BF16),
-        state, state, state, state, state,
+        travel, state, state, travel, travel,
         pltpu.VMEM((n_mp, 1, width), F32),
         pltpu.VMEM((rows, 1), F32),
         pltpu.SMEM((seq_dev * seqs,), F32),

time: 97.1 us -> 92.8 us (0.956)
  Pallas kernels: 96.9 us -> 92.6 us
    pallas_call x1, Pallas kernels: 91 us -> 86.7 us  [fused(): pl.pallas_call(functools.partial(core_kernel, n_dp, n_mp, streams, full_w...]
where the time goes in v5:
time: 92.8 us; the launch traced here: 92.6 us
  Pallas kernels  92.6 us (100%)
    pallas_call x1, Pallas kernels, fused(): pl.pallas_call(functools.partial(core_kernel, n_dp, n_mp, streams, full_w...  86.7 us
    pallas_call x1, Pallas kernels, fused(): pl.pallas_call(grad_kernel, grid=(pl.cdiv(width, tile),), out_shape=jax.S...  5.94 us

profile of v5, /device:TPU:0, one launch (start us, length us, event | category | flops | bytes accessed | tf_op | source)
XLA Modules:
  0.0 92.6 jit_solution(15424963456732165572)
XLA Ops:
  0.0 86.7 %shard_map.73 = (bf16[2,2,4,48,660]{4,3,2,1,0:T(8,128)(2,1)}, bf16[2,2,2,4,48,660]{5,4,3,2,1,0:T(8,128)(2,1)}) custom-call(s32[12]{0:T(128)} %counts_in.1, s32[12]{0:T(128)} %groups_in.1, bf16[3,32,660]{2,1,0:T(8,128)(2,1)} %prelude_ref.1, bf16[4,32,660]{2,1,0:T(8,128)(2,1)} %noise_ref.1, bf16[4,32,660]{2,1,0:T(8,128)(2,1)} %cot_ref.1, f32[5280]{0:T(1024)} %gain_in.1, ...), custom_call_target="tpu_custom_call" | custom-call | flops 2676326400 | bytes 20000000 | tf_op jit(solution)/shard_map/pallas_call | solution.py:674
  86.7 5.9 %shard_map.74 = f32[660,1320]{1,0:T(8,128)} custom-call(bf16[2,2,4,48,660]{4,3,2,1,0:T(8,128)(2,1)} %get-tuple-element.7.ds_ref, bf16[2,2,2,4,48,660]{5,4,3,2,1,0:T(8,128)(2,1)} %get-tuple-element.8.xs_ref), custom_call_target="tpu_custom_call" | custom-call | tf_op jit(solution)/shard_map/pallas_call | solution.py:694

commit v6 on v5

--- a/solution.py
+++ b/solution.py
@@ -270,6 +270,10 @@
         ).start()
 
     def gather_steps(turn, s, buf, use, forwarded=False):
+        if not forwarded:
+            for h in range(1, n_line):
+                gather_forward(turn, s, buf, h)
+
         def step(at, carry):
             h = jnp.where(at < 2, 0, jnp.where(at <= n_line, at - 1, at - n_line))
             other = jnp.where(at < 2, at, jnp.where(at <= n_line, 0, 1))
@@ -278,12 +282,6 @@
             @pl.when((at == 1) | (at > n_line))
             def _():
                 gather_wait(turn, s, buf, at, owner)
-
-            if not forwarded:
-
-                @pl.when((at >= 2) & (at <= n_line))
-                def _():
-                    gather_forward(turn, s, buf, h)
 
             use(owner)
             return carry

time: 92.8 us -> 91 us (0.981)
  Pallas kernels: 92.6 us -> 90.8 us
    pallas_call x1, Pallas kernels: 86.7 us -> 84.9 us  [fused(): pl.pallas_call(functools.partial(core_kernel, n_dp, n_mp, streams, full_w...]
where the time goes in v6:
time: 91 us; the launch traced here: 90.8 us
  Pallas kernels  90.8 us (100%)
    pallas_call x1, Pallas kernels, fused(): pl.pallas_call(functools.partial(core_kernel, n_dp, n_mp, streams, full_w...  84.9 us
    pallas_call x1, Pallas kernels, fused(): pl.pallas_call(grad_kernel, grid=(pl.cdiv(width, tile),), out_shape=jax.S...  5.94 us

profile of v6, /device:TPU:0, one launch (start us, length us, event | category | flops | bytes accessed | tf_op | source)
XLA Modules:
  0.0 90.8 jit_solution(7043060140374899987)
XLA Ops:
  0.0 84.9 %shard_map.73 = (bf16[2,2,4,48,660]{4,3,2,1,0:T(8,128)(2,1)}, bf16[2,2,2,4,48,660]{5,4,3,2,1,0:T(8,128)(2,1)}) custom-call(s32[12]{0:T(128)} %counts_in.1, s32[12]{0:T(128)} %groups_in.1, bf16[3,32,660]{2,1,0:T(8,128)(2,1)} %prelude_ref.1, bf16[4,32,660]{2,1,0:T(8,128)(2,1)} %noise_ref.1, bf16[4,32,660]{2,1,0:T(8,128)(2,1)} %cot_ref.1, f32[5280]{0:T(1024)} %gain_in.1, ...), custom_call_target="tpu_custom_call" | custom-call | flops 2676326400 | bytes 20000000 | tf_op jit(solution)/shard_map/pallas_call | solution.py:672
  84.9 5.9 %shard_map.74 = f32[660,1320]{1,0:T(8,128)} custom-call(bf16[2,2,4,48,660]{4,3,2,1,0:T(8,128)(2,1)} %get-tuple-element.7.ds_ref, bf16[2,2,2,4,48,660]{5,4,3,2,1,0:T(8,128)(2,1)} %get-tuple-element.8.xs_ref), custom_call_target="tpu_custom_call" | custom-call | tf_op jit(solution)/shard_map/pallas_call | solution.py:692

commit v7 on v6

--- a/solution.py
+++ b/solution.py
@@ -269,10 +269,13 @@
             buf.at[s, owner], buf.at[s, owner], g_send.at[turn, s, at], g_recv.at[turn, s, at], peer
         ).start()
 
+    def gather_forwards(turn, s, buf):
+        for h in range(1, n_line):
+            gather_forward(turn, s, buf, h)
+
     def gather_steps(turn, s, buf, use, forwarded=False):
         if not forwarded:
-            for h in range(1, n_line):
-                gather_forward(turn, s, buf, h)
+            gather_forwards(turn, s, buf)
 
         def step(at, carry):
             h = jnp.where(at < 2, 0, jnp.where(at <= n_line, at - 1, at - n_line))
@@ -363,7 +366,7 @@
     for s in range(streams):
         first(s, s == 0)
 
-    def renew(turn, s, y_all, old_block, after):
+    def renew(turn, s, y_all, old_block, after, forwarded=False):
         live = active(turn, s)
         acc[s] = jnp.zeros((part_rows, width), F32)
         square[...] = jnp.zeros_like(square)
@@ -389,7 +392,7 @@
                     (to, mp),
                 ).start()
 
-        gather_steps(1 + turn, s, y_all, use)
+        gather_steps(1 + turn, s, y_all, use, forwarded=forwarded)
         root = lax.rsqrt(square[...] / full_width + EPS)
         rms[turn, rows_of(s)] = root
         previous = 1.0 if turn == 0 else scale[turn - 1, rows_of(s)]
@@ -438,13 +441,11 @@
         columns = jnp.transpose(total)
         return columns[:, 0:1], columns[:, 4:5]
 
-    def third(s):
-        renew(1, s, y1, lambda k: u1[s, k].astype(F32), u2)
+    def third(s, forwarded):
+        renew(1, s, y1, lambda k: u1[s, k].astype(F32), u2, forwarded=forwarded)
         y = (scale[1, rows_of(s)] * acc[s] + inject[rows_of(s)]).astype(BF16).astype(F32)
         y_last[rows_of(s)] = y
         sums_start(0, s, (y * y, scaled[rows_of(s)] * y))
-
-    each_stream(third)
 
     dp_pair, dp_side = dp // 2, lax.rem(dp, 2)
     n_pair = n_dp // 2
@@ -518,8 +519,6 @@
         inner = delta_b[s].astype(F32) * acc[s]
         sums_start(1, s, (inner,))
 
-    each_stream(back_first)
-
     def back_second(s):
         def line_step(at, carry):
             to_line = lax.rem(line + at + 1, n_line)
@@ -537,7 +536,14 @@
 
         lax.fori_loop(0, n_line, line_step, 0)
 
-    each_stream(back_second)
+    third(0, False)
+    for s in range(1, streams):
+        gather_forwards(2, s, y1)
+        back_first(s - 1)
+        third(s, True)
+        back_second(s - 1)
+    back_first(streams - 1)
+    back_second(streams - 1)
     for s in range(streams):
         spread_forward(1, s)
 

time: 91 us -> 91 us (level)
  no operation moved by 1% of the time
where the time goes in v7:
time: 91 us; the launch traced here: 90.8 us
  Pallas kernels  90.8 us (100%)
    pallas_call x1, Pallas kernels, fused(): pl.pallas_call(functools.partial(core_kernel, n_dp, n_mp, streams, full_w...  84.9 us
    pallas_call x1, Pallas kernels, fused(): pl.pallas_call(grad_kernel, grid=(pl.cdiv(width, tile),), out_shape=jax.S...  5.95 us

profile of v7, /device:TPU:0, one launch (start us, length us, event | category | flops | bytes accessed | tf_op | source)
XLA Modules:
  0.0 90.8 jit_solution(986401171353452293)
XLA Ops:
  0.0 84.9 %shard_map.73 = (bf16[2,2,4,48,660]{4,3,2,1,0:T(8,128)(2,1)}, bf16[2,2,2,4,48,660]{5,4,3,2,1,0:T(8,128)(2,1)}) custom-call(s32[12]{0:T(128)} %counts_in.1, s32[12]{0:T(128)} %groups_in.1, bf16[3,32,660]{2,1,0:T(8,128)(2,1)} %prelude_ref.1, bf16[4,32,660]{2,1,0:T(8,128)(2,1)} %noise_ref.1, bf16[4,32,660]{2,1,0:T(8,128)(2,1)} %cot_ref.1, f32[5280]{0:T(1024)} %gain_in.1, ...), custom_call_target="tpu_custom_call" | custom-call | flops 2676326400 | bytes 20000000 | tf_op jit(solution)/shard_map/pallas_call | solution.py:678
  84.9 6.0 %shard_map.74 = f32[660,1320]{1,0:T(8,128)} custom-call(bf16[2,2,4,48,660]{4,3,2,1,0:T(8,128)(2,1)} %get-tuple-element.7.ds_ref, bf16[2,2,2,4,48,660]{5,4,3,2,1,0:T(8,128)(2,1)} %get-tuple-element.8.xs_ref), custom_call_target="tpu_custom_call" | custom-call | tf_op jit(solution)/shard_map/pallas_call | solution.py:698
